TPU v7x, 256 devices: a whole 4x4x8 slice. The times are simulated.
256 devices in a mesh: seq: 64 (over z_hi, x, y), grp: 4 (over z_lo, core).
Axes of the slice: x: 4, y: 4, z: 8 (z_hi: 4, z_lo: 2; z = z_hi * 2 + z_lo), core: 2. Of those that a mesh axis runs over, the one named last changes fastest.
Arguments:
- block_query_rows: bfloat16 [4096, 8192], P(('seq', 'grp')), may hold values from -400 to 400
- block_key_rows: bfloat16 [4096, 1024], P(('seq', 'grp')), may hold values from -6 to 6
- block_value_rows: bfloat16 [4096, 1024], P(('seq', 'grp')), may hold values from -6 to 6
- stretch_pos: int32 [4096], replicated, may hold values from 0 to 4095, each once
- prompt_key_cache: bfloat16 [8192, 1024], P(('seq', 'grp')), may hold values from -6 to 6
- prompt_value_cache: bfloat16 [8192, 1024], P(('seq', 'grp')), may hold values from -6 to 6
- embed_table: bfloat16 [65536, 8192], P('grp', 'seq'), may hold values from -6 to 6
- query_weight: bfloat16 [8192, 8192], P('seq', 'grp'), may hold values from -64 to 64
- key_weight: bfloat16 [8192, 1024], P('seq', 'grp'), may hold values from -0.0625 to 0.0625
- value_weight: bfloat16 [8192, 1024], P('seq', 'grp'), may hold values from -0.0625 to 0.0625
- beam_tokens: int32 [128, 2], replicated, may hold values from 0 to 65535
- parent_beam: int32 [128], replicated, may hold values from 0 to 127
Outputs:
- stretch_attn: bfloat16 [4096, 8192], P('seq', 'grp')
- decode_attn: bfloat16 [128, 2, 8192], P('seq', None, 'grp')
Inputs may be any that keep to these rules, and one draw needn't show every extreme that they name: `stretch_pos`: a permutation of 0 to 4095.
All inputs are finite; a program needn't handle non-finite values.
Results may differ from a plain program's by a relative error of at most 0.01155.
Values may be sent and summed in bfloat16 or wider, within the bound.
No kernel may reach another device: no remote copies, remote signals or barrier semaphores. Data moves between devices by JAX's collectives and lax.ppermute only.
A program may use at most 192 MiB of HBM per device.

v0:
```python
import jax
import jax.numpy as jnp
import numpy as np
from jax import lax
from jax.experimental import pallas as pl
from jax.experimental.pallas import tpu as pltpu
from jax.sharding import Mesh, PartitionSpec as P

HEAD = 128
GROUP = 8
WIDTH = GROUP * HEAD
EXP2_SCALE = HEAD ** (-0.5) * 1.4426950408889634
HIDE = -1e30
ALL = ("zh", "x", "y", "zl", "c")
SEQ = ("zh", "x", "y")
GRP = ("zl", "c")
DEPTH = ("zh", "zl")
OLD, NEW = 32, 16
BOTH = OLD + NEW
TOKENS = 8 * NEW
BEAMS = 8
TILES = 11 * BEAMS
STATS = 32
MESSAGE = WIDTH + HEAD
VMEM = pltpu.CompilerParams(vmem_limit_bytes=56 * 1024 * 1024)
SMEM_SPEC = pl.BlockSpec(memory_space=pltpu.SMEM)
VMEM_SPEC = pl.BlockSpec(memory_space=pltpu.VMEM)
BF16, F32 = jnp.bfloat16, jnp.float32


def dot_nt(a, b):
    return lax.dot_general(a, b, (((1,), (1,)), ((), ())), preferred_element_type=F32)


def dot_nn(a, b):
    return lax.dot_general(a, b, (((1,), (0,)), ((), ())), preferred_element_type=F32)


def call(kernel, out_shape, scalars, args, name, cost=None, scratch=()):
    return pl.pallas_call(
        kernel,
        out_shape=out_shape,
        in_specs=[SMEM_SPEC] * len(scalars) + [VMEM_SPEC] * len(args),
        out_specs=jax.tree.map(lambda _: VMEM_SPEC, out_shape),
        scratch_shapes=list(scratch),
        cost_estimate=cost,
        compiler_params=VMEM,
        name=name,
    )(*scalars, *args)


def head_of(plane):
    return 4 * (plane & 1) + 2 * ((plane >> 1) & 1) + (plane >> 2)


def pack_kernel(core, old_k, old_v, new_k, new_v, q, wq, wk, wv, out, *w_out):
    for plane in range(8):
        head = head_of(plane)
        cols = slice(head * HEAD, (head + 1) * HEAD)
        out[plane, :OLD, :HEAD] = old_k[:, cols]
        out[plane, :OLD, HEAD:] = old_v[:, cols]
        out[plane, OLD:BOTH, :HEAD] = new_k[:, cols]
        out[plane, OLD:BOTH, HEAD:] = new_v[:, cols]
        for pair in range(4):
            at = head * WIDTH + pair * 2 * HEAD
            out[plane, BOTH + pair * NEW : BOTH + (pair + 1) * NEW, :] = q[:, at : at + 2 * HEAD]
    for k in range(4):
        part = core[2] ^ k
        w_out[k][:, : 4 * HEAD] = wq[:, pl.ds(pl.multiple_of(part * 4 * HEAD, 4 * HEAD), 4 * HEAD)]
        cols = pl.ds(pl.multiple_of((part // 2) * HEAD, HEAD), HEAD)
        w_out[k][:, 4 * HEAD :] = jnp.where(part % 2 == 0, wk[:, cols], wv[:, cols])


def hidden_kernel(core, owner, *refs):
    looked, out = refs[:4], refs[4]
    rows = jnp.zeros(out.shape, F32)
    for k in range(4):
        rows = rows + jnp.where(owner[...] == (core[3] ^ k), looked[k][...].astype(F32), 0.0)
    out[...] = rows.astype(BF16)


def project_kernel(parent, beam_id, *refs):
    hidden, weights, (out, total, extra) = refs[:4], refs[4:8], refs[8:]
    beams = extra.shape[0]
    pick = jnp.where(parent[...] == beam_id[...], 1.0, 0.0).astype(BF16)
    acc = acc_extra = 0.0
    for k in range(4):
        rows = hidden[k][...]
        acc = acc + dot_nn(rows, weights[k][...])
        chosen = dot_nn(pick, rows[:beams]).astype(BF16)
        acc_extra = acc_extra + dot_nn(chosen, weights[k][:, 4 * HEAD :])
    total[...] = acc
    extra[...] = acc_extra
    for chip in range(16):
        for step in range(2):
            rows = slice(step * beams + chip * BEAMS, step * beams + (chip + 1) * BEAMS)
            for head in range(4):
                at = (step * 4 + head) * BEAMS
                out[chip, at : at + BEAMS, :] = total[rows, head * HEAD : (head + 1) * HEAD]
            at = (8 + step) * BEAMS
            out[chip, at : at + BEAMS, :] = total[rows, 4 * HEAD :]
        out[chip, 10 * BEAMS :, :] = extra[chip * BEAMS : (chip + 1) * BEAMS, :]


def sum_kernel(parts, out):
    terms = [parts[i] for i in range(parts.shape[0])]
    while len(terms) > 1:
        terms = [a + b for a, b in zip(terms[::2], terms[1::2])]
    out[...] = terms[0]


def spread(ref, row):
    return jnp.transpose(jnp.broadcast_to(ref[row : row + 1, :], (TOKENS, HEAD)))


def load_lines(pair):
    wide = []
    for low, high in ((0, OLD), (OLD, BOTH)):
        count = 16 * (high - low)
        k = jnp.concatenate([r[:, :, low:high, :HEAD].reshape(count, HEAD) for r in pair], 0)
        v = jnp.concatenate([r[:, :, low:high, HEAD:].reshape(count, HEAD) for r in pair], 0)
        wide.append((k, jnp.concatenate([v, jnp.ones_like(v)], 1)))
    return wide


def absorb(state, tiles, wide):
    peak = jnp.maximum(
        jnp.max(tiles[0], axis=-1, keepdims=True), jnp.max(tiles[1], axis=-1, keepdims=True)
    )
    if state is None:
        peak = jnp.broadcast_to(peak, (TOKENS, HEAD))
    else:
        top, total, acc = state
        peak = jnp.maximum(top, peak)
        alpha = jnp.exp2((top - peak) * EXP2_SCALE)
    mixed = 0.0
    for s, (_, v) in zip(tiles, wide):
        w = jnp.exp2((s - peak[:, :1]) * EXP2_SCALE).astype(BF16)
        mixed = mixed + dot_nn(w, v)
    if state is None:
        return peak, mixed[:, HEAD:], mixed[:, :HEAD]
    return peak, mixed[:, HEAD:] + total * alpha, mixed[:, :HEAD] + acc * alpha


def put_state(ref, slot, state):
    top, total, acc = state
    ref[slot * TOKENS : (slot + 1) * TOKENS, :] = acc
    at = ref.shape[0] - STATS + slot
    ref[at : at + 1, :] = jnp.transpose(top)[:1]
    at = at + STATS // 2
    ref[at : at + 1, :] = jnp.transpose(total)[:1]


def get_state(ref, slot):
    at = ref.shape[0] - STATS + slot
    rows = slice(slot * TOKENS, (slot + 1) * TOKENS)
    return spread(ref, at), spread(ref, at + STATS // 2), ref[rows, :]


def attend_kernel(starts, resumed, earlier, core, pos, lines, own, other, *refs):
    if earlier:
        mine, theirs, refs = refs[0], refs[1], refs[2:]
    if resumed:
        states, refs = refs[:2], refs[2:]
    kv, (keep, send) = refs[:-2], refs[-2:]
    me, place = core[0], core[1]

    def column(which):
        row = pos[pl.ds(which * 16 + place, 1), :].astype(F32)
        return jnp.transpose(jnp.broadcast_to(row, (TOKENS, HEAD)))[:, :1]

    qpos = (column(me), column(1 - me))
    loaded = {}
    if earlier:
        halves, beams = beam_queries(me, mine, theirs)

    def scores(step, block):
        if step not in loaded and step < 0:
            first, part, _ = earlier[step]
            pair = [r.at[4 * part : 4 * part + 4] for r in kv[first : first + 2]]
            loaded[step] = (load_lines(pair), None)
        if step not in loaded:
            first, part, line = starts[step]
            kpos = jnp.concatenate([lines[line : line + 1], lines[4 + line : 5 + line]], 1)
            kpos = kpos.astype(F32)
            bias = [jnp.where(kpos <= p, 0.0, HIDE) for p in qpos]
            pair = [r.at[4 * part : 4 * part + 4] for r in kv[first : first + 2]]
            loaded[step] = (load_lines(pair), bias)
        wide, bias = loaded[step]
        if block == 2 * GROUP:
            return [dot_nt(beams, k) for k, _ in wide]
        head = block % GROUP
        lanes = slice((head % 2) * HEAD, (head % 2 + 1) * HEAD)
        at = BOTH + (head // 2) * NEW
        q = (own, other)[block // GROUP][:, at : at + NEW, lanes].reshape(TOKENS, HEAD)
        return dot_nt(q, wide[0][0]), dot_nt(q, wide[1][0]) + bias[block // GROUP]

    state = {}
    blocks = 2 * GROUP + (1 if earlier else 0)
    order = [(step - len(earlier), 2 * GROUP) for step in range(len(earlier))]
    order += [(step, block) for step in range(len(starts)) for block in range(blocks)]
    ahead = scores(*order[0])
    for i, (step, block) in enumerate(order):
        now = ahead
        if i + 1 < len(order):
            ahead = scores(*order[i + 1])
        if step == 0 and resumed and block < 2 * GROUP:
            state[block] = get_state(states[block // GROUP], block % GROUP)
        state[block] = absorb(state.get(block), now, loaded[step][0])
        if step == len(starts) - 1:
            if block < 2 * GROUP:
                put_state((keep, send)[block // GROUP], block % GROUP, state[block])
            else:
                for ref in (keep, send):
                    put_state(ref, GROUP, absorb_own(me, halves, beams, state[block]))


def beam_queries(me, mine, theirs):
    halves = [jnp.where(me == 0, mine[...], theirs[...]), jnp.where(me == 0, theirs[...], mine[...])]
    return halves, jnp.concatenate([h[: 8 * BEAMS] for h in halves], 0).astype(BF16)


def absorb_own(me, halves, queries, state):
    top, total, acc = state
    count = 4 * BEAMS
    pad = jnp.zeros((count - 3 * BEAMS, HEAD), F32)
    own_k = jnp.concatenate([halves[0][8 * BEAMS :], pad], 0).astype(BF16)
    own_v = jnp.concatenate([halves[1][8 * BEAMS :], pad], 0).astype(BF16)
    row = lax.broadcasted_iota(jnp.int32, (TOKENS, count), 0)
    key = lax.broadcasted_iota(jnp.int32, (TOKENS, count), 1)
    step = (row // (4 * BEAMS)) % 2
    beam = row % BEAMS
    slot = key // BEAMS
    first = jnp.logical_and(step == 0, slot == 0)
    second = jnp.logical_and(step == 1, jnp.logical_or(slot == 1, slot == 2))
    seen = jnp.logical_and(beam == key % BEAMS, jnp.logical_or(first, second))
    seen = jnp.logical_and(seen, beam // 4 == me)
    own = jnp.where(seen, dot_nt(queries, own_k), HIDE)
    peak = jnp.maximum(top, jnp.max(own, axis=-1, keepdims=True))
    alpha = jnp.exp2((top - peak) * EXP2_SCALE)
    w = jnp.exp2((own - peak[:, :1]) * EXP2_SCALE)
    total = total * alpha + jnp.sum(w, axis=-1, keepdims=True)
    acc = acc * alpha + dot_nn(w.astype(BF16), own_v)
    return peak, total, acc


def merge_kernel(core, keep, got, out, message):
    me = core[0]
    for zh in range(4):
        message[zh, NEW:, WIDTH:] = jnp.zeros((NEW, HEAD), F32)
    for slot in range(GROUP + 1):
        parts = [get_state(ref, slot) for ref in (keep, got)]
        peak = jnp.maximum(parts[0][0], parts[1][0])
        a, b = [jnp.exp2((p[0] - peak) * EXP2_SCALE) for p in parts]
        total = parts[0][1] * a + parts[1][1] * b
        mixed = (parts[0][2] * a + parts[1][2] * b) / total
        if slot < GROUP:
            lanes = slice(slot * HEAD, (slot + 1) * HEAD)
            for zh in range(4):
                message[zh, :, lanes] = mixed[zh * 2 * NEW : (zh + 1) * 2 * NEW]
        else:
            for block in range(16):
                half, step, head = block // 8, (block // 4) % 2, block % 4
                at = step * GROUP + half * 4 + head
                tile = mixed[block * BEAMS : (block + 1) * BEAMS]
                tile = jnp.where(me == 0, tile[:4], tile[4:])
                for zh in range(4):
                    message[zh, at : at + 1, WIDTH:] = tile[zh : zh + 1]
    out[...] = message[...].astype(BF16)


def place_kernel(core, near, far, stretch, decode):
    me = core[0]
    for j in range(2):
        lanes = slice(j * WIDTH, (j + 1) * WIDTH)
        own, other = near[2 * j + me], far[2 * j + me]
        for side, parity in ((own, me), (other, 1 - me)):
            for low in range(2):
                row = pl.multiple_of(low * 2 * NEW + parity * NEW, NEW)
                stretch[pl.ds(row, NEW), lanes] = side[low * NEW : (low + 1) * NEW, :WIDTH]
        tails = [v[:NEW, WIDTH:].astype(F32) for v in (own, other)]
        for parity in range(2):
            few = jnp.where(me == parity, tails[0], tails[1])
            steps = [
                jnp.concatenate([few[s * GROUP + g : s * GROUP + g + 1] for g in range(GROUP)], 1)
                for s in range(2)
            ]
            decode[parity, :, lanes] = jnp.concatenate(steps, 0).astype(BF16)


def shards(
    block_query_rows,
    block_key_rows,
    block_value_rows,
    stretch_pos,
    prompt_key_cache,
    prompt_value_cache,
    embed_table,
    query_weight,
    key_weight,
    value_weight,
    beam_tokens,
    parent_beam,
):
    xi, yi, ci = (lax.axis_index(a) for a in ("x", "y", "c"))
    core = jnp.stack([ci, xi * 4 + yi, xi, lax.axis_index(GRP)])
    core = core.astype(jnp.int32)

    depth = query_weight.shape[0]
    q_cols = query_weight.shape[1] // 4
    packed, *weights = call(
        pack_kernel,
        (
            jax.ShapeDtypeStruct((8, BOTH + 4 * NEW, 2 * HEAD), BF16),
            *[jax.ShapeDtypeStruct((depth, q_cols + HEAD), BF16)] * 4,
        ),
        (core,),
        (
            prompt_key_cache,
            prompt_value_cache,
            block_key_rows,
            block_value_rows,
            block_query_rows,
            query_weight,
            key_weight,
            value_weight,
        ),
        "pack",
    )
    packed = lax.all_to_all(packed, DEPTH, split_axis=0, concat_axis=0, tiled=True)

    def cross(v, axis, k):
        return lax.ppermute(v, axis, [(i, i ^ k) for i in range(4)])

    weights = [weights[0]] + [cross(weights[k], "x", k) for k in (1, 2, 3)]

    vocab_rows = embed_table.shape[0]
    beams = beam_tokens.shape[0]
    ids = jnp.transpose(beam_tokens.reshape(4, 4, 4, 2, 2), (4, 1, 2, 3, 0)).reshape(-1)
    looked = embed_table.at[ids % vocab_rows].get(mode="promise_in_bounds")
    looked = [looked] + [cross(looked, GRP, k) for k in (1, 2, 3)]
    weights, looked = lax.optimization_barrier((weights, looked))

    def swap(v, axis, turn):
        pairs = []
        for at in range(8):
            i, c = at // 2, at % 2
            pairs.append((at, (i ^ (1 if c == turn else 3)) * 2 + c))
        return lax.ppermute(v, (axis, "c"), pairs)

    halves = [packed[:4, :BOTH][None], packed[4:, :BOTH][None]]
    got = [swap(half, axis, 0) for half, axis in zip(halves, ("x", "y"))]
    got, looked = lax.optimization_barrier((got, looked))
    halves = [jnp.concatenate(pair, 0) for pair in zip(halves, got)]
    near = [
        jnp.concatenate([half, swap(half, axis, 1)], 0) for half, axis in zip(halves, ("x", "y"))
    ]
    packed_other = lax.ppermute(packed, "c", [(0, 1), (1, 0)])

    pos = jnp.transpose(stretch_pos.reshape(4, 4, 4, 2, 2, NEW), (4, 1, 2, 0, 3, 5))
    halves = lax.dynamic_index_in_dim(pos.reshape(2, 4, 4, 2, TOKENS // 2), ci, 0, keepdims=False)
    pos = pos.reshape(32, TOKENS)

    def met(table, axis, index):
        table = jnp.moveaxis(table, axis, 0)
        table = jnp.where(index % 2 == 1, jnp.concatenate([table[1:2], table[:1], table[3:], table[2:3]], 0), table)
        table = jnp.where(index // 2 == 1, jnp.concatenate([table[2:], table[:2]], 0), table)
        one, three = jnp.where(ci == 0, table[1], table[3]), jnp.where(ci == 0, table[3], table[1])
        return jnp.moveaxis(jnp.stack([table[0], one, three, table[2]]), 0, axis)

    halves = met(met(halves, 0, xi), 1, yi)
    line_pos = jnp.concatenate(
        [
            jnp.transpose(halves[:, :, 0], (1, 0, 2)).reshape(4, 2 * TOKENS),
            halves[:, :, 1].reshape(4, 2 * TOKENS),
        ],
        0,
    )

    hidden = call(
        hidden_kernel,
        jax.ShapeDtypeStruct((2 * beams, HEAD), BF16),
        (core,),
        ((ids // vocab_rows)[:, None], *looked),
        "hidden",
    )
    hidden = [hidden] + [cross(hidden, "x", k) for k in (1, 2, 3)]

    near, hidden = lax.optimization_barrier((near, hidden))
    far = [swap(line, axis, 0) for line, axis in zip(near, ("y", "x"))]
    both = [jnp.concatenate(pair, 0) for pair in zip(near, far)]

    beam_id = np.arange(beams, dtype=np.int32).reshape(4, 4, 4, 2).transpose(1, 2, 3, 0)
    parent = jnp.transpose(parent_beam.reshape(4, 4, 4, 2), (1, 2, 3, 0))
    part = call(
        project_kernel,
        jax.ShapeDtypeStruct((16, TILES, HEAD), F32),
        (),
        (parent.reshape(-1, 1), beam_id.reshape(1, -1), *hidden, *weights),
        "project",
        scratch=[
            pltpu.VMEM((2 * beams, q_cols + HEAD), F32),
            pltpu.VMEM((beams, HEAD), F32),
        ],
    )
    part, both = lax.optimization_barrier((part, both))
    rest = [swap(line, axis, 1) for line, axis in zip(both, ("y", "x"))]
    part = lax.all_to_all(part, ("zh", "y"), split_axis=0, concat_axis=0, tiled=True)
    def attend(starts, carry, pieces, name, earlier=(), beam_rows=()):
        work = 2 * GROUP * TOKENS * len(starts) * 32 * BOTH
        slots = GROUP + (1 if earlier else 0)
        state = jax.ShapeDtypeStruct((slots * TOKENS + STATS, HEAD), F32)
        return call(
            lambda *refs: attend_kernel(starts, bool(carry), earlier, *refs),
            (state, state),
            (core,),
            (pos, line_pos, packed, packed_other, *beam_rows, *carry, *pieces),
            name,
            cost=pl.CostEstimate(
                flops=8 * work * HEAD, bytes_accessed=work // 4, transcendentals=work
            ),
        )

    carry = attend(((0, 0, 0), (2, 0, 1)), (), near + far, "attend_near")
    carry, part = lax.optimization_barrier((carry, part))
    part = call(sum_kernel, jax.ShapeDtypeStruct((TILES, HEAD), F32), (), (part,), "sum")
    sides = []
    for i in range(2):
        pairs = []
        for at in range(64):
            h, j, p, l, c = at >> 4, (at >> 3) & 1, (at >> 2) & 1, (at >> 1) & 1, at & 1
            pairs.append((at, (((2 * j + c) * 4 + h) * 2 + l) * 2 + (p ^ i)))
        sides.append(lax.ppermute(part, ("zh", "x", "zl", "c"), pairs))
    keep, send = attend(
        ((4, 0, 2), (4, 1, 3)),
        carry,
        near + far + rest,
        "attend_rest",
        earlier=((0, 0, 0), (2, 0, 1)),
        beam_rows=sides,
    )
    got = lax.ppermute(send, "c", [(0, 1), (1, 0)])
    messages = call(
        merge_kernel,
        jax.ShapeDtypeStruct((4, 2 * NEW, MESSAGE), BF16),
        (core,),
        (keep, got),
        "merge",
        scratch=[pltpu.VMEM((4, 2 * NEW, MESSAGE), F32)],
    )

    near = lax.all_to_all(messages, "zh", split_axis=0, concat_axis=0, tiled=True)
    far = lax.ppermute(near, "c", [(0, 1), (1, 0)])
    return call(
        place_kernel,
        (
            jax.ShapeDtypeStruct((4 * NEW, 2 * WIDTH), BF16),
            jax.ShapeDtypeStruct((2, 2, 2 * WIDTH), BF16),
        ),
        (core,),
        (near, far),
        "place",
    )


def solution(mesh):
    fine = Mesh(mesh.devices.reshape(4, 4, 4, 2, 2), ALL)
    return jax.shard_map(
        shards,
        mesh=fine,
        in_specs=(
            P(ALL, None),
            P(ALL, None),
            P(ALL, None),
            P(),
            P(ALL, None),
            P(ALL, None),
            P(GRP, SEQ),
            P(SEQ, GRP),
            P(SEQ, GRP),
            P(SEQ, GRP),
            P(),
            P(),
        ),
        out_specs=(P(SEQ, GRP), P(SEQ, None, GRP)),
        check_vma=False,
    )
```

profile of v0, /device:TPU:1, one launch (start us, length us, event | category | flops | bytes accessed | tf_op | source)
XLA Modules:
  0.0 144.8 jit_solution(17078883195452933993)
XLA Ops:
  1.2 2.3 %pack.1 = (bf16[8,112,256]{2,1,0:T(8,128)(2,1)}, bf16[128,640]{1,0:T(8,128)(2,1)}, bf16[128,640]{1,0:T(8,128)(2,1)}, bf16[128,640]{1,0:T(8,128)(2,1)}, bf16[128,640]{1,0:T(8,128)(2,1)}) custom-call(s32[4]{0:T(128)} %pad_add_fusion.1.core.refs_0_, bf16[32,1024]{1,0:T(8,128)(2,1)} %old_k.1, bf16[32,1024]{1,0:T(8,128)(2,1)} %old_v.1, bf16[16,1024]{1,0:T(8,128)(2,1)} %new_k.1, ...), custom_call_target="tpu_custom_call" | custom-call | tf_op jit(solution)/shard_map/pack/pallas_call | solution.py:40
  3.5 9.0 %all-to-all-start = ((bf16[8,112,256]{2,1,0:T(8,128)(2,1)}), bf16[8,112,256]{2,1,0:T(8,128)(2,1)S(1)}, u32[]{:S(2)}, u32[]{:S(2)}) async-start(bf16[8,112,256]{2,1,0:T(8,128)(2,1)} %get-tuple-element.37), calls=%async_computation | async-start | bytes 917504 | tf_op jit(solution)/shard_map/all_to_all | solution.py:330
  12.5 0.8 reshape.147
  13.8 0.8 add_select_fusion
  14.6 3.5 %gather_fusion = bf16[256,128]{1,0:T(8,128)(2,1)S(1)} fusion(bf16[16384,128]{1,0:T(8,128)(2,1)} %param.19, s32[1024]{0:T(1024)S(1)} %pad_clamp_fusion), kind=kCustom, calls=%fused_computation | custom fusion | bytes 132096 | tf_op jit(solution)/shard_map/gather | solution.py:340
  18.1 2.7 %collective-permute-start.8 = (bf16[256,128]{1,0:T(8,128)(2,1)S(1)}, bf16[256,128]{1,0:T(8,128)(2,1)S(1)}, u32[]{:S(2)}, u32[]{:S(2)}) collective-permute-start(bf16[256,128]{1,0:T(8,128)(2,1)S(1)} %gather_fusion), channel_id=1, source_target_pairs={{0,3},{1,2},{2,1},{3,0},{4,7},{5,6},{6,5},{7,4},{8,11},{9,10},{10,... | collective-permute-start | bytes 196616 | tf_op jit(solution)/shard_map/ppermute | solution.py:333
  21.2 1.2 collective-permute-start.3
  22.4 2.5 %collective-permute-start.4 = (bf16[128,640]{1,0:T(8,128)(2,1)}, bf16[128,640]{1,0:T(8,128)(2,1)S(1)}, u32[]{:S(2)}, u32[]{:S(2)}) collective-permute-start(bf16[128,640]{1,0:T(8,128)(2,1)} %get-tuple-element.40), channel_id=1, source_target_pairs={{0,32},{16,48},{32,0},{48,16},{1,33},{17,49},{33,1},{49,17},{2,34}... | collective-permute-start | bytes 491528 | tf_op jit(solution)/shard_map/ppermute | solution.py:333
  24.9 0.9 reshape.143
  26.2 2.2 %all-to-all-done.refs_3_ = bf16[8,112,256]{2,1,0:T(8,128)(2,1)S(1)} async-done(((bf16[8,112,256]{2,1,0:T(8,128)(2,1)}), bf16[8,112,256]{2,1,0:T(8,128)(2,1)S(1)}, u32[]{:S(2)}, u32[]{:S(2)}) %all-to-all-start) | async-done | bytes 458784 | tf_op jit(solution)/shard_map/all_to_all | solution.py:330
  28.5 2.6 %collective-permute-start.5 = (bf16[128,640]{1,0:T(8,128)(2,1)}, bf16[128,640]{1,0:T(8,128)(2,1)S(1)}, u32[]{:S(2)}, u32[]{:S(2)}) collective-permute-start(bf16[128,640]{1,0:T(8,128)(2,1)} %get-tuple-element.41), channel_id=1, source_target_pairs={{0,48},{16,32},{32,16},{48,0},{1,49},{17,33},{33,17},{49,1},{2,50}... | collective-permute-start | bytes 491528 | tf_op jit(solution)/shard_map/ppermute | solution.py:333
  31.0 2.7 %collective-permute-start.2 = (bf16[1,4,48,256]{3,2,1,0:T(8,128)(2,1)S(1)}, bf16[1,4,48,256]{3,2,1,0:T(8,128)(2,1)S(1)}, u32[]{:S(2)}, u32[]{:S(2)}) collective-permute-start(bf16[1,4,48,256]{3,2,1,0:T(8,128)(2,1)S(1)} %get-tuple-element.72), channel_id=1, source_target_pairs={{0,4},{1,13},{4,0},{5,9},{8,12},{9,5},{12,8},{13,1},{2,6},{3,15},{... | collective-permute-start | bytes 294920 | tf_op jit(solution)/shard_map/ppermute | solution.py:349
  34.0 1.9 %collective-permute-done.5.refs_7_ = bf16[128,640]{1,0:T(8,128)(2,1)S(1)} collective-permute-done((bf16[128,640]{1,0:T(8,128)(2,1)}, bf16[128,640]{1,0:T(8,128)(2,1)S(1)}, u32[]{:S(2)}, u32[]{:S(2)}) %collective-permute-start.5) | collective-permute-done | bytes 163872 | tf_op jit(solution)/shard_map/ppermute | solution.py:333
  36.1 2.4 %collective-permute-done.1 = bf16[1,4,48,256]{3,2,1,0:T(8,128)(2,1)S(1)} collective-permute-done((bf16[1,4,48,256]{3,2,1,0:T(8,128)(2,1)S(1)}, bf16[1,4,48,256]{3,2,1,0:T(8,128)(2,1)S(1)}, u32[]{:S(2)}, u32[]{:S(2)}) %collective-permute-start.1) | collective-permute-done | bytes 98336 | tf_op jit(solution)/shard_map/ppermute | solution.py:349
  39.4 1.8 %hidden.1.refs_0_ = bf16[256,128]{1,0:T(8,128)(2,1)} custom-call(s32[4]{0:T(128)} %pad_add_fusion.1.core.refs_0_, s32[256,1]{1,0:T(8,128)} %get-tuple-element.74.owner, bf16[256,128]{1,0:T(8,128)(2,1)} %copy-done.9, bf16[256,128]{1,0:T(8,128)(2,1)} %copy-done.18, bf16[256,128]{1,0:T(8,128)(2,1)} %copy-done.17, bf16[256,128]{1,0:T(8,128)(2,1)} %copy-done.16), custom_call_target="tpu_custom_call" | custom-call | tf_op jit(solution)/shard_map/hidden/pallas_call | solution.py:40
  41.3 1.2 collective-permute-start.13
  42.5 1.8 %collective-permute-start.12 = (bf16[256,128]{1,0:T(8,128)(2,1)}, bf16[256,128]{1,0:T(8,128)(2,1)S(1)}, u32[]{:S(2)}, u32[]{:S(2)}) collective-permute-start(bf16[256,128]{1,0:T(8,128)(2,1)} %hidden.1.refs_0_), channel_id=1, source_target_pairs={{0,32},{16,48},{32,0},{48,16},{1,33},{17,49},{33,1},{49,17},{2,34}... | collective-permute-start | bytes 196616 | tf_op jit(solution)/shard_map/ppermute | solution.py:333
  44.7 1.7 %collective-permute-done.13.refs_3_ = bf16[256,128]{1,0:T(8,128)(2,1)S(1)} collective-permute-done((bf16[256,128]{1,0:T(8,128)(2,1)}, bf16[256,128]{1,0:T(8,128)(2,1)S(1)}, u32[]{:S(2)}, u32[]{:S(2)}) %collective-permute-start.13) | collective-permute-done | bytes 65568 | tf_op jit(solution)/shard_map/ppermute | solution.py:333
  46.4 1.0 collective-permute-done.12.refs_2_
  47.9 1.4 collective-permute-start.15
  49.4 1.6 %collective-permute-start.14 = (bf16[4,4,48,256]{3,2,1,0:T(8,128)(2,1)S(1)}, bf16[4,4,48,256]{3,2,1,0:T(8,128)(2,1)S(1)}, u32[]{:S(2)}, u32[]{:S(2)}) collective-permute-start(bf16[4,4,48,256]{3,2,1,0:T(8,128)(2,1)S(1)} %pad_maximum_fusion.2.refs_5_.refs_9_), channel_id=1, source_target_pairs={{0,4},{1,13},{4,0},{5,9},{8,12},{9,5},{12,8},{13,1},{2,6},{3,15},{... | collective-permute-start | bytes 1179656 | tf_op jit(solution)/shard_map/ppermute | solution.py:349
  51.4 0.7 reshape.160.parent
  52.2 3.1 %project.1 = f32[16,88,128]{2,1,0:T(8,128)} custom-call(s32[128,1]{1,0:T(8,128)} %reshape.160.parent, s32[1,128]{1,0:T(1,128)} %constant.87.clone.beam_id, bf16[256,128]{1,0:T(8,128)(2,1)} %hidden.1.refs_0_, bf16[256,128]{1,0:T(8,128)(2,1)} %copy-done.15, bf16[256,128]{1,0:T(8,128)(2,1)} %copy-done.14, bf16[256,128]{1,0:T(8,128)(2,1)} %copy-done.13, ...), custom_call_target="tpu_custom_call" | custom-call | tf_op jit(solution)/shard_map/project/pallas_call | solution.py:40
  55.2 0.9 collective-permute-done.15.refs_8_.refs_12_
  56.2 1.0 collective-permute-done.14.refs_7_.refs_11_
  57.2 1.0 pad_maximum_fusion
  58.2 7.9 %all-to-all-start.1 = ((f32[16,88,128]{2,1,0:T(8,128)}), f32[16,88,128]{2,1,0:T(8,128)S(1)}, u32[]{:S(2)}, u32[]{:S(2)}) async-start(f32[16,88,128]{2,1,0:T(8,128)} %project.1), calls=%async_computation.1 | async-start | bytes 1441792 | tf_op jit(solution)/shard_map/all_to_all | solution.py:408
  66.2 1.6 %collective-permute-start = (bf16[8,112,256]{2,1,0:T(8,128)(2,1)S(1)}, bf16[8,112,256]{2,1,0:T(8,128)(2,1)}, u32[]{:S(2)}, u32[]{:S(2)}) collective-permute-start(bf16[8,112,256]{2,1,0:T(8,128)(2,1)S(1)} %all-to-all-done.refs_3_), channel_id=1, source_target_pairs={{0,1},{1,0},{2,3},{3,2},{4,5},{5,4},{6,7},{7,6},{8,9},{9,8},{10,11... | collective-permute-start | bytes 1376264 | tf_op jit(solution)/shard_map/ppermute | solution.py:358
  67.8 1.7 %collective-permute-start.18 = (bf16[8,4,48,256]{3,2,1,0:T(8,128)(2,1)}, bf16[8,4,48,256]{3,2,1,0:T(8,128)(2,1)}, u32[]{:S(2)}, u32[]{:S(2)}) collective-permute-start(bf16[8,4,48,256]{3,2,1,0:T(8,128)(2,1)} %pad_maximum_fusion), channel_id=1, source_target_pairs={{0,12},{1,5},{4,8},{5,1},{8,4},{9,13},{12,0},{13,9},{2,14},{3,7},{... | collective-permute-start | bytes 2359304 | tf_op jit(solution)/shard_map/ppermute | solution.py:349
  69.6 1.5 %collective-permute-start.19 = (bf16[8,4,48,256]{3,2,1,0:T(8,128)(2,1)S(1)}, bf16[8,4,48,256]{3,2,1,0:T(8,128)(2,1)}, u32[]{:S(2)}, u32[]{:S(2)}) collective-permute-start(bf16[8,4,48,256]{3,2,1,0:T(8,128)(2,1)S(1)} %pad_maximum_fusion.1), channel_id=1, source_target_pairs={{0,48},{1,17},{16,32},{17,1},{32,16},{33,49},{48,0},{49,33},{2,50}... | collective-permute-start | bytes 2359304 | tf_op jit(solution)/shard_map/ppermute | solution.py:349
  71.1 0.8 reshape.144.refs_1_
  72.7 10.6 %attend_near.1 = (f32[1056,128]{1,0:T(8,128)}, f32[1056,128]{1,0:T(8,128)}) custom-call(s32[4]{0:T(128)} %pad_add_fusion.1.core.refs_0_, s32[32,128]{1,0:T(8,128)} %reshape.144.refs_1_, s32[8,256]{1,0:T(8,128)} %pad_add_fusion.refs_2_, bf16[8,112,256]{2,1,0:T(8,128)(2,1)} %copy-done.4, bf16[8,112,256]{2,1,0:T(8,128)(2,1)} %collective-permute-done.refs_4_, ...), custom_call_target="tpu_custom_call" | custom-call | flops 6442450944 | bytes 1572864 | tf_op jit(solution)/shard_map/attend_near/pallas_call | solution.py:40
  83.3 3.4 %all-to-all-done.1.parts = f32[16,88,128]{2,1,0:T(8,128)S(1)} async-done(((f32[16,88,128]{2,1,0:T(8,128)}), f32[16,88,128]{2,1,0:T(8,128)S(1)}, u32[]{:S(2)}, u32[]{:S(2)}) %all-to-all-start.1) | async-done | bytes 720928 | tf_op jit(solution)/shard_map/all_to_all | solution.py:408
  86.6 0.9 copy-done
  87.5 1.8 %sum.1 = f32[88,128]{1,0:T(8,128)} custom-call(f32[16,88,128]{2,1,0:T(8,128)} %copy-done), custom_call_target="tpu_custom_call" | custom-call | tf_op jit(solution)/shard_map/sum/pallas_call | solution.py:40
  89.2 2.8 %collective-permute-start.17 = (f32[88,128]{1,0:T(8,128)}, f32[88,128]{1,0:T(8,128)S(1)}, u32[]{:S(2)}, u32[]{:S(2)}) collective-permute-start(f32[88,128]{1,0:T(8,128)} %sum.1), channel_id=1, source_target_pairs={{0,1},{1,65},{2,3},{3,67},{16,0},{17,64},{18,2},{19,66},{32,129},{... | collective-permute-start | bytes 135176 | tf_op jit(solution)/shard_map/ppermute | solution.py:433
  92.1 3.0 %collective-permute-start.16 = (f32[88,128]{1,0:T(8,128)}, f32[88,128]{1,0:T(8,128)S(1)}, u32[]{:S(2)}, u32[]{:S(2)}) collective-permute-start(f32[88,128]{1,0:T(8,128)} %sum.1), channel_id=1, source_target_pairs={{0,0},{1,64},{2,2},{3,66},{16,1},{17,65},{18,3},{19,67},{32,128},{... | collective-permute-start | bytes 135176 | tf_op jit(solution)/shard_map/ppermute | solution.py:433
  95.1 2.5 %collective-permute-done.16.refs_5_ = f32[88,128]{1,0:T(8,128)S(1)} collective-permute-done((f32[88,128]{1,0:T(8,128)}, f32[88,128]{1,0:T(8,128)S(1)}, u32[]{:S(2)}, u32[]{:S(2)}) %collective-permute-start.16) | collective-permute-done | bytes 45088 | tf_op jit(solution)/shard_map/ppermute | solution.py:433
  97.6 0.6 copy-done.21
  98.3 12.8 %attend_rest.1 = (f32[1184,128]{1,0:T(8,128)}, f32[1184,128]{1,0:T(8,128)}) custom-call(s32[4]{0:T(128)} %pad_add_fusion.1.core.refs_0_, s32[32,128]{1,0:T(8,128)} %reshape.144.refs_1_, s32[8,256]{1,0:T(8,128)} %pad_add_fusion.refs_2_, bf16[8,112,256]{2,1,0:T(8,128)(2,1)} %copy-done.4, bf16[8,112,256]{2,1,0:T(8,128)(2,1)} %collective-permute-done.refs_4_, ...), custom_call_target="tpu_custom_call" | custom-call | flops 6442450944 | bytes 1572864 | tf_op jit(solution)/shard_map/attend_rest/pallas_call | solution.py:40
  111.1 2.2 %collective-permute-done.20.got = f32[1184,128]{1,0:T(8,128)S(1)} collective-permute-done((f32[1184,128]{1,0:T(8,128)}, f32[1184,128]{1,0:T(8,128)S(1)}, u32[]{:S(2)}, u32[]{:S(2)}) %collective-permute-start.20) | collective-permute-done | bytes 606240 | tf_op jit(solution)/shard_map/ppermute | solution.py:442
  113.3 0.8 copy-done.5
  114.2 2.7 %merge.1 = bf16[4,32,1152]{2,1,0:T(8,128)(2,1)} custom-call(s32[4]{0:T(128)} %pad_add_fusion.1.core.refs_0_, f32[1184,128]{1,0:T(8,128)} %get-tuple-element.70.keep, f32[1184,128]{1,0:T(8,128)} %copy-done.5), custom_call_target="tpu_custom_call" | custom-call | tf_op jit(solution)/shard_map/merge/pallas_call | solution.py:40
  116.9 22.4 %all_to_all.15.near = bf16[4,32,1152]{2,1,0:T(8,128)(2,1)S(1)} all-to-all(bf16[4,32,1152]{2,1,0:T(8,128)(2,1)} %merge.1), channel_id=1, replica_groups=mesh['zh'=4,'x'=4,'y'=4,'zl'=2,'c'=2] {'zh'}, dimensions={0} | all-to-all | bytes 589824 | tf_op jit(solution)/shard_map/all_to_all | solution.py:452
  139.3 1.7 %collective-permute-start.21 = (bf16[4,32,1152]{2,1,0:T(8,128)(2,1)S(1)}, bf16[4,32,1152]{2,1,0:T(8,128)(2,1)S(1)}, u32[]{:S(2)}, u32[]{:S(2)}) collective-permute-start(bf16[4,32,1152]{2,1,0:T(8,128)(2,1)S(1)} %all_to_all.15.near), channel_id=1, source_target_pairs={{0,1},{1,0},{2,3},{3,2},{4,5},{5,4},{6,7},{7,6},{8,9},{9,8},{10,11... | collective-permute-start | bytes 884744 | tf_op jit(solution)/shard_map/ppermute | solution.py:453
  141.0 1.2 collective-permute-done.21.far
  142.2 0.7 copy-done.8
  143.0 1.8 %place.1 = (bf16[64,2048]{1,0:T(8,128)(2,1)}, bf16[2,2,2048]{2,1,0:T(2,128)(2,1)}) custom-call(s32[4]{0:T(128)} %pad_add_fusion.1.core.refs_0_, bf16[4,32,1152]{2,1,0:T(8,128)(2,1)} %copy-done.3, bf16[4,32,1152]{2,1,0:T(8,128)(2,1)} %copy-done.8), custom_call_target="tpu_custom_call" | custom-call | tf_op jit(solution)/shard_map/place/pallas_call | solution.py:40
  (92 shorter events, 5.3 us)
Async XLA Ops:
  0.6 50.4 %copy-start.19 = (s32[128]{0:T(128)S(1)}, s32[128]{0:T(128)}, u32[]{:S(2)}) copy-start(s32[128]{0:T(128)} %param.24) | copy-start | bytes 1540
  3.5 24.9 %all-to-all-start = ((bf16[8,112,256]{2,1,0:T(8,128)(2,1)}), bf16[8,112,256]{2,1,0:T(8,128)(2,1)S(1)}, u32[]{:S(2)}, u32[]{:S(2)}) async-start(bf16[8,112,256]{2,1,0:T(8,128)(2,1)} %get-tuple-element.37), calls=%async_computation | async-start | bytes 917504 | tf_op jit(solution)/shard_map/all_to_all | solution.py:330
  18.1 21.3 %copy-start.9 = (bf16[256,128]{1,0:T(8,128)(2,1)}, bf16[256,128]{1,0:T(8,128)(2,1)S(1)}, u32[]{:S(2)}) copy-start(bf16[256,128]{1,0:T(8,128)(2,1)S(1)} %gather_fusion) | copy-start | bytes 196612
  18.1 10.4 %collective-permute-start.8 = (bf16[256,128]{1,0:T(8,128)(2,1)S(1)}, bf16[256,128]{1,0:T(8,128)(2,1)S(1)}, u32[]{:S(2)}, u32[]{:S(2)}) collective-permute-start(bf16[256,128]{1,0:T(8,128)(2,1)S(1)} %gather_fusion), channel_id=1, source_target_pairs={{0,3},{1,2},{2,1},{3,0},{4,7},{5,6},{6,5},{7,4},{8,11},{9,10},{10,... | collective-permute-start | bytes 196616 | tf_op jit(solution)/shard_map/ppermute | solution.py:333
  20.7 10.3 %collective-permute-start.7 = (bf16[256,128]{1,0:T(8,128)(2,1)S(1)}, bf16[256,128]{1,0:T(8,128)(2,1)S(1)}, u32[]{:S(2)}, u32[]{:S(2)}) collective-permute-start(bf16[256,128]{1,0:T(8,128)(2,1)S(1)} %gather_fusion), channel_id=1, source_target_pairs={{0,2},{1,3},{2,0},{3,1},{4,6},{5,7},{6,4},{7,5},{8,10},{9,11},{10,... | collective-permute-start | bytes 196616 | tf_op jit(solution)/shard_map/ppermute | solution.py:333
  20.7 13.0 %collective-permute-start.6 = (bf16[256,128]{1,0:T(8,128)(2,1)S(1)}, bf16[256,128]{1,0:T(8,128)(2,1)S(1)}, u32[]{:S(2)}, u32[]{:S(2)}) collective-permute-start(bf16[256,128]{1,0:T(8,128)(2,1)S(1)} %gather_fusion), channel_id=1, source_target_pairs={{0,1},{1,0},{2,3},{3,2},{4,5},{5,4},{6,7},{7,6},{8,9},{9,8},{10,11... | collective-permute-start | bytes 196616 | tf_op jit(solution)/shard_map/ppermute | solution.py:333
  21.2 12.7 %collective-permute-start.3 = (bf16[128,640]{1,0:T(8,128)(2,1)}, bf16[128,640]{1,0:T(8,128)(2,1)S(1)}, u32[]{:S(2)}, u32[]{:S(2)}) collective-permute-start(bf16[128,640]{1,0:T(8,128)(2,1)} %get-tuple-element.39), channel_id=1, source_target_pairs={{0,16},{16,0},{32,48},{48,32},{1,17},{17,1},{33,49},{49,33},{2,18}... | collective-permute-start | bytes 491528 | tf_op jit(solution)/shard_map/ppermute | solution.py:333
  22.4 11.5 %collective-permute-start.4 = (bf16[128,640]{1,0:T(8,128)(2,1)}, bf16[128,640]{1,0:T(8,128)(2,1)S(1)}, u32[]{:S(2)}, u32[]{:S(2)}) collective-permute-start(bf16[128,640]{1,0:T(8,128)(2,1)} %get-tuple-element.40), channel_id=1, source_target_pairs={{0,32},{16,48},{32,0},{48,16},{1,33},{17,49},{33,1},{49,17},{2,34}... | collective-permute-start | bytes 491528 | tf_op jit(solution)/shard_map/ppermute | solution.py:333
  28.4 37.8 %copy-start.4 = (bf16[8,112,256]{2,1,0:T(8,128)(2,1)}, bf16[8,112,256]{2,1,0:T(8,128)(2,1)S(1)}, u32[]{:S(2)}) copy-start(bf16[8,112,256]{2,1,0:T(8,128)(2,1)S(1)} %all-to-all-done.refs_3_) | copy-start | bytes 1376260
  28.4 11.0 %copy-start.16 = (bf16[256,128]{1,0:T(8,128)(2,1)}, bf16[256,128]{1,0:T(8,128)(2,1)S(1)}, u32[]{:S(2)}) copy-start(bf16[256,128]{1,0:T(8,128)(2,1)S(1)} %collective-permute-done.8.refs_3_) | copy-start | bytes 196612
  28.5 7.4 %collective-permute-start.5 = (bf16[128,640]{1,0:T(8,128)(2,1)}, bf16[128,640]{1,0:T(8,128)(2,1)S(1)}, u32[]{:S(2)}, u32[]{:S(2)}) collective-permute-start(bf16[128,640]{1,0:T(8,128)(2,1)} %get-tuple-element.41), channel_id=1, source_target_pairs={{0,48},{16,32},{32,16},{48,0},{1,49},{17,33},{33,17},{49,1},{2,50}... | collective-permute-start | bytes 491528 | tf_op jit(solution)/shard_map/ppermute | solution.py:333
  31.0 8.4 %copy-start.17 = (bf16[256,128]{1,0:T(8,128)(2,1)}, bf16[256,128]{1,0:T(8,128)(2,1)S(1)}, u32[]{:S(2)}) copy-start(bf16[256,128]{1,0:T(8,128)(2,1)S(1)} %collective-permute-done.7.refs_2_) | copy-start | bytes 196612
  31.0 5.0 %collective-permute-start.2 = (bf16[1,4,48,256]{3,2,1,0:T(8,128)(2,1)S(1)}, bf16[1,4,48,256]{3,2,1,0:T(8,128)(2,1)S(1)}, u32[]{:S(2)}, u32[]{:S(2)}) collective-permute-start(bf16[1,4,48,256]{3,2,1,0:T(8,128)(2,1)S(1)} %get-tuple-element.72), channel_id=1, source_target_pairs={{0,4},{1,13},{4,0},{5,9},{8,12},{9,5},{12,8},{13,1},{2,6},{3,15},{... | collective-permute-start | bytes 294920 | tf_op jit(solution)/shard_map/ppermute | solution.py:349
  33.8 5.7 %copy-start.18 = (bf16[256,128]{1,0:T(8,128)(2,1)}, bf16[256,128]{1,0:T(8,128)(2,1)S(1)}, u32[]{:S(2)}) copy-start(bf16[256,128]{1,0:T(8,128)(2,1)S(1)} %collective-permute-done.6.refs_1_) | copy-start | bytes 196612
  33.8 4.7 %collective-permute-start.1 = (bf16[1,4,48,256]{3,2,1,0:T(8,128)(2,1)S(1)}, bf16[1,4,48,256]{3,2,1,0:T(8,128)(2,1)S(1)}, u32[]{:S(2)}, u32[]{:S(2)}) collective-permute-start(bf16[1,4,48,256]{3,2,1,0:T(8,128)(2,1)S(1)} %get-tuple-element.73), channel_id=1, source_target_pairs={{0,16},{1,49},{16,0},{17,33},{32,48},{33,17},{48,32},{49,1},{2,18}... | collective-permute-start | bytes 294920 | tf_op jit(solution)/shard_map/ppermute | solution.py:349
  34.0 18.2 %copy-start.10 = (bf16[128,640]{1,0:T(8,128)(2,1)}, bf16[128,640]{1,0:T(8,128)(2,1)S(1)}, u32[]{:S(2)}) copy-start(bf16[128,640]{1,0:T(8,128)(2,1)S(1)} %collective-permute-done.3.refs_5_) | copy-start | bytes 491524
  34.0 18.1 %copy-start.11 = (bf16[128,640]{1,0:T(8,128)(2,1)}, bf16[128,640]{1,0:T(8,128)(2,1)S(1)}, u32[]{:S(2)}) copy-start(bf16[128,640]{1,0:T(8,128)(2,1)S(1)} %collective-permute-done.4.refs_6_) | copy-start | bytes 491524
  35.9 16.2 %copy-start.12 = (bf16[128,640]{1,0:T(8,128)(2,1)}, bf16[128,640]{1,0:T(8,128)(2,1)S(1)}, u32[]{:S(2)}) copy-start(bf16[128,640]{1,0:T(8,128)(2,1)S(1)} %collective-permute-done.5.refs_7_) | copy-start | bytes 491524
  38.5 6.1 %collective-permute-start.10 = (bf16[2,4,48,256]{3,2,1,0:T(8,128)(2,1)S(1)}, bf16[2,4,48,256]{3,2,1,0:T(8,128)(2,1)S(1)}, u32[]{:S(2)}, u32[]{:S(2)}) collective-permute-start(bf16[2,4,48,256]{3,2,1,0:T(8,128)(2,1)S(1)} %pad_maximum_fusion.5), channel_id=1, source_target_pairs={{0,12},{1,5},{4,8},{5,1},{8,4},{9,13},{12,0},{13,9},{2,14},{3,7},{... | collective-permute-start | bytes 589832 | tf_op jit(solution)/shard_map/ppermute | solution.py:349
  39.1 5.5 %collective-permute-start.9 = (bf16[2,4,48,256]{3,2,1,0:T(8,128)(2,1)S(1)}, bf16[2,4,48,256]{3,2,1,0:T(8,128)(2,1)S(1)}, u32[]{:S(2)}, u32[]{:S(2)}) collective-permute-start(bf16[2,4,48,256]{3,2,1,0:T(8,128)(2,1)S(1)} %pad_maximum_fusion.4), channel_id=1, source_target_pairs={{0,48},{1,17},{16,32},{17,1},{32,16},{33,49},{48,0},{49,33},{2,50}... | collective-permute-start | bytes 589832 | tf_op jit(solution)/shard_map/ppermute | solution.py:349
  41.3 5.1 %collective-permute-start.13 = (bf16[256,128]{1,0:T(8,128)(2,1)}, bf16[256,128]{1,0:T(8,128)(2,1)S(1)}, u32[]{:S(2)}, u32[]{:S(2)}) collective-permute-start(bf16[256,128]{1,0:T(8,128)(2,1)} %hidden.1.refs_0_), channel_id=1, source_target_pairs={{0,48},{16,32},{32,16},{48,0},{1,49},{17,33},{33,17},{49,1},{2,50}... | collective-permute-start | bytes 196616 | tf_op jit(solution)/shard_map/ppermute | solution.py:333
  42.5 4.9 %collective-permute-start.12 = (bf16[256,128]{1,0:T(8,128)(2,1)}, bf16[256,128]{1,0:T(8,128)(2,1)S(1)}, u32[]{:S(2)}, u32[]{:S(2)}) collective-permute-start(bf16[256,128]{1,0:T(8,128)(2,1)} %hidden.1.refs_0_), channel_id=1, source_target_pairs={{0,32},{16,48},{32,0},{48,16},{1,33},{17,49},{33,1},{49,17},{2,34}... | collective-permute-start | bytes 196616 | tf_op jit(solution)/shard_map/ppermute | solution.py:333
  44.3 3.6 %collective-permute-start.11 = (bf16[256,128]{1,0:T(8,128)(2,1)}, bf16[256,128]{1,0:T(8,128)(2,1)S(1)}, u32[]{:S(2)}, u32[]{:S(2)}) collective-permute-start(bf16[256,128]{1,0:T(8,128)(2,1)} %hidden.1.refs_0_), channel_id=1, source_target_pairs={{0,16},{16,0},{32,48},{48,32},{1,17},{17,1},{33,49},{49,33},{2,18}... | collective-permute-start | bytes 196616 | tf_op jit(solution)/shard_map/ppermute | solution.py:333
  44.6 28.1 %copy-start.1 = (bf16[4,4,48,256]{3,2,1,0:T(8,128)(2,1)}, bf16[4,4,48,256]{3,2,1,0:T(8,128)(2,1)S(1)}, u32[]{:S(2)}) copy-start(bf16[4,4,48,256]{3,2,1,0:T(8,128)(2,1)S(1)} %pad_maximum_fusion.3.refs_6_.refs_10_) | copy-start | bytes 1179652
  44.7 28.0 %copy-start.2 = (bf16[4,4,48,256]{3,2,1,0:T(8,128)(2,1)}, bf16[4,4,48,256]{3,2,1,0:T(8,128)(2,1)S(1)}, u32[]{:S(2)}) copy-start(bf16[4,4,48,256]{3,2,1,0:T(8,128)(2,1)S(1)} %pad_maximum_fusion.2.refs_5_.refs_9_) | copy-start | bytes 1179652
  46.4 5.7 %copy-start.13 = (bf16[256,128]{1,0:T(8,128)(2,1)}, bf16[256,128]{1,0:T(8,128)(2,1)S(1)}, u32[]{:S(2)}) copy-start(bf16[256,128]{1,0:T(8,128)(2,1)S(1)} %collective-permute-done.13.refs_3_) | copy-start | bytes 196612
  47.5 4.7 %copy-start.14 = (bf16[256,128]{1,0:T(8,128)(2,1)}, bf16[256,128]{1,0:T(8,128)(2,1)S(1)}, u32[]{:S(2)}) copy-start(bf16[256,128]{1,0:T(8,128)(2,1)S(1)} %collective-permute-done.12.refs_2_) | copy-start | bytes 196612
  47.9 4.2 %copy-start.15 = (bf16[256,128]{1,0:T(8,128)(2,1)}, bf16[256,128]{1,0:T(8,128)(2,1)S(1)}, u32[]{:S(2)}) copy-start(bf16[256,128]{1,0:T(8,128)(2,1)S(1)} %collective-permute-done.11.refs_1_) | copy-start | bytes 196612
  47.9 8.2 %collective-permute-start.15 = (bf16[4,4,48,256]{3,2,1,0:T(8,128)(2,1)S(1)}, bf16[4,4,48,256]{3,2,1,0:T(8,128)(2,1)S(1)}, u32[]{:S(2)}, u32[]{:S(2)}) collective-permute-start(bf16[4,4,48,256]{3,2,1,0:T(8,128)(2,1)S(1)} %pad_maximum_fusion.3.refs_6_.refs_10_), channel_id=1, source_target_pairs={{0,16},{1,49},{16,0},{17,33},{32,48},{33,17},{48,32},{49,1},{2,18}... | collective-permute-start | bytes 1179656 | tf_op jit(solution)/shard_map/ppermute | solution.py:349
  49.4 7.8 %collective-permute-start.14 = (bf16[4,4,48,256]{3,2,1,0:T(8,128)(2,1)S(1)}, bf16[4,4,48,256]{3,2,1,0:T(8,128)(2,1)S(1)}, u32[]{:S(2)}, u32[]{:S(2)}) collective-permute-start(bf16[4,4,48,256]{3,2,1,0:T(8,128)(2,1)S(1)} %pad_maximum_fusion.2.refs_5_.refs_9_), channel_id=1, source_target_pairs={{0,4},{1,13},{4,0},{5,9},{8,12},{9,5},{12,8},{13,1},{2,6},{3,15},{... | collective-permute-start | bytes 1179656 | tf_op jit(solution)/shard_map/ppermute | solution.py:349
  56.1 16.5 %copy-start.6 = (bf16[4,4,48,256]{3,2,1,0:T(8,128)(2,1)}, bf16[4,4,48,256]{3,2,1,0:T(8,128)(2,1)S(1)}, u32[]{:S(2)}) copy-start(bf16[4,4,48,256]{3,2,1,0:T(8,128)(2,1)S(1)} %collective-permute-done.15.refs_8_.refs_12_) | copy-start | bytes 1179652
  57.2 1.0 copy-start.7
  58.2 28.4 %all-to-all-start.1 = ((f32[16,88,128]{2,1,0:T(8,128)}), f32[16,88,128]{2,1,0:T(8,128)S(1)}, u32[]{:S(2)}, u32[]{:S(2)}) async-start(f32[16,88,128]{2,1,0:T(8,128)} %project.1), calls=%async_computation.1 | async-start | bytes 1441792 | tf_op jit(solution)/shard_map/all_to_all | solution.py:408
  66.2 6.5 %collective-permute-start = (bf16[8,112,256]{2,1,0:T(8,128)(2,1)S(1)}, bf16[8,112,256]{2,1,0:T(8,128)(2,1)}, u32[]{:S(2)}, u32[]{:S(2)}) collective-permute-start(bf16[8,112,256]{2,1,0:T(8,128)(2,1)S(1)} %all-to-all-done.refs_3_), channel_id=1, source_target_pairs={{0,1},{1,0},{2,3},{3,2},{4,5},{5,4},{6,7},{7,6},{8,9},{9,8},{10,11... | collective-permute-start | bytes 1376264 | tf_op jit(solution)/shard_map/ppermute | solution.py:358
  67.8 27.2 %collective-permute-start.18 = (bf16[8,4,48,256]{3,2,1,0:T(8,128)(2,1)}, bf16[8,4,48,256]{3,2,1,0:T(8,128)(2,1)}, u32[]{:S(2)}, u32[]{:S(2)}) collective-permute-start(bf16[8,4,48,256]{3,2,1,0:T(8,128)(2,1)} %pad_maximum_fusion), channel_id=1, source_target_pairs={{0,12},{1,5},{4,8},{5,1},{8,4},{9,13},{12,0},{13,9},{2,14},{3,7},{... | collective-permute-start | bytes 2359304 | tf_op jit(solution)/shard_map/ppermute | solution.py:349
  69.6 25.5 %collective-permute-start.19 = (bf16[8,4,48,256]{3,2,1,0:T(8,128)(2,1)S(1)}, bf16[8,4,48,256]{3,2,1,0:T(8,128)(2,1)}, u32[]{:S(2)}, u32[]{:S(2)}) collective-permute-start(bf16[8,4,48,256]{3,2,1,0:T(8,128)(2,1)S(1)} %pad_maximum_fusion.1), channel_id=1, source_target_pairs={{0,48},{1,17},{16,32},{17,1},{32,16},{33,49},{48,0},{49,33},{2,50}... | collective-permute-start | bytes 2359304 | tf_op jit(solution)/shard_map/ppermute | solution.py:349
  86.6 0.9 copy-start
  89.2 5.9 %collective-permute-start.17 = (f32[88,128]{1,0:T(8,128)}, f32[88,128]{1,0:T(8,128)S(1)}, u32[]{:S(2)}, u32[]{:S(2)}) collective-permute-start(f32[88,128]{1,0:T(8,128)} %sum.1), channel_id=1, source_target_pairs={{0,1},{1,65},{2,3},{3,67},{16,0},{17,64},{18,2},{19,66},{32,129},{... | collective-permute-start | bytes 135176 | tf_op jit(solution)/shard_map/ppermute | solution.py:433
  92.1 5.6 %collective-permute-start.16 = (f32[88,128]{1,0:T(8,128)}, f32[88,128]{1,0:T(8,128)S(1)}, u32[]{:S(2)}, u32[]{:S(2)}) collective-permute-start(f32[88,128]{1,0:T(8,128)} %sum.1), channel_id=1, source_target_pairs={{0,0},{1,64},{2,2},{3,66},{16,1},{17,65},{18,3},{19,67},{32,128},{... | collective-permute-start | bytes 135176 | tf_op jit(solution)/shard_map/ppermute | solution.py:433
  95.1 2.5 %copy-start.20 = (f32[88,128]{1,0:T(8,128)}, f32[88,128]{1,0:T(8,128)S(1)}, u32[]{:S(2)}) copy-start(f32[88,128]{1,0:T(8,128)S(1)} %collective-permute-done.17.refs_6_) | copy-start | bytes 135172
  97.6 0.6 copy-start.21
  111.1 2.2 %collective-permute-start.20 = (f32[1184,128]{1,0:T(8,128)}, f32[1184,128]{1,0:T(8,128)S(1)}, u32[]{:S(2)}, u32[]{:S(2)}) collective-permute-start(f32[1184,128]{1,0:T(8,128)} %get-tuple-element.71), channel_id=1, source_target_pairs={{0,1},{1,0},{2,3},{3,2},{4,5},{5,4},{6,7},{7,6},{8,9},{9,8},{10,11... | collective-permute-start | bytes 1818632 | tf_op jit(solution)/shard_map/ppermute | solution.py:442
  113.3 0.8 copy-start.5
  139.3 2.9 %copy-start.3 = (bf16[4,32,1152]{2,1,0:T(8,128)(2,1)}, bf16[4,32,1152]{2,1,0:T(8,128)(2,1)S(1)}, u32[]{:S(2)}) copy-start(bf16[4,32,1152]{2,1,0:T(8,128)(2,1)S(1)} %all_to_all.15.near) | copy-start | bytes 884740
  139.3 2.9 %collective-permute-start.21 = (bf16[4,32,1152]{2,1,0:T(8,128)(2,1)S(1)}, bf16[4,32,1152]{2,1,0:T(8,128)(2,1)S(1)}, u32[]{:S(2)}, u32[]{:S(2)}) collective-permute-start(bf16[4,32,1152]{2,1,0:T(8,128)(2,1)S(1)} %all_to_all.15.near), channel_id=1, source_target_pairs={{0,1},{1,0},{2,3},{3,2},{4,5},{5,4},{6,7},{7,6},{8,9},{9,8},{10,11... | collective-permute-start | bytes 884744 | tf_op jit(solution)/shard_map/ppermute | solution.py:453
  142.2 0.7 copy-start.8
where the time goes:
time: 145 us
  starting transfers between devices  48.8 us (34%)
  Pallas kernels  36.9 us (25%)
  blocking collectives  22.4 us (15%)
  waiting for transfers between devices  21.2 us (15%)
  local copies, waits for them, and re-layouts  11.1 us (8%)
  other arithmetic  3.26 us (2%)
    pallas_call x8, Pallas kernels, call(): pl.pallas_call(kernel, out_shape=out_shape, in_specs=[SMEM_SPEC] * len(sc...  36.9 us
    all_to_all x1, blocking collectives, shards(): lax.all_to_all(messages, 'zh', split_axis=0, concat_axis=0, tiled=True)  22.4 us
    ppermute x9, starting transfers between devices, cross(): return lax.ppermute(v, axis, [(i, i ^ k) for i in range(4)])  12.6 us
    ppermute x8, starting transfers between devices, swap(): return lax.ppermute(v, (axis, 'c'), pairs)  10.1 us
    all_to_all x1, starting transfers between devices, shards(): lax.all_to_all(packed, DEPTH, split_axis=0, concat_axis=0, tiled=True)  9.01 us
    all_to_all x1, starting transfers between devices, shards(): lax.all_to_all(part, ('zh', 'y'), split_axis=0, concat_axis=0, tiled=True)  7.9 us
    ppermute x2, starting transfers between devices, shards(): sides.append(lax.ppermute(part, ('zh', 'x', 'zl', 'c'), pairs))  5.82 us
    ppermute x9, waiting for transfers between devices, cross(): return lax.ppermute(v, axis, [(i, i ^ k) for i in range(4)])  5.17 us
  transfers between devices with their start and end apart: 24, of which 13 were waited for; matrix products, arithmetic and copies ran while one was open for 7% of the time, Pallas kernels for 12%

commit v1 on v0

--- a/solution.py
+++ b/solution.py
@@ -71,18 +71,26 @@
         w_out[k][:, 4 * HEAD :] = jnp.where(part % 2 == 0, wk[:, cols], wv[:, cols])
 
 
+def spread(ref, row):
+    return jnp.transpose(jnp.broadcast_to(ref[row : row + 1, :].astype(F32), (TOKENS, HEAD)))
+
+
 def hidden_kernel(core, owner, *refs):
     looked, out = refs[:4], refs[4]
-    rows = jnp.zeros(out.shape, F32)
-    for k in range(4):
-        rows = rows + jnp.where(owner[...] == (core[3] ^ k), looked[k][...].astype(F32), 0.0)
-    out[...] = rows.astype(BF16)
+    for part in range(owner.shape[0]):
+        at = slice(part * HEAD, (part + 1) * HEAD)
+        who = spread(owner, part)
+        rows = jnp.zeros((HEAD, HEAD), F32)
+        for k in range(4):
+            from_k = (core[3] ^ k).astype(F32)
+            rows = rows + jnp.where(who == from_k, looked[k][at, :].astype(F32), 0.0)
+        out[at, :] = rows.astype(BF16)
 
 
 def project_kernel(parent, beam_id, *refs):
     hidden, weights, (out, total, extra) = refs[:4], refs[4:8], refs[8:]
     beams = extra.shape[0]
-    pick = jnp.where(parent[...] == beam_id[...], 1.0, 0.0).astype(BF16)
+    pick = jnp.where(spread(parent, 0) == beam_id[...].astype(F32), 1.0, 0.0).astype(BF16)
     acc = acc_extra = 0.0
     for k in range(4):
         rows = hidden[k][...]
@@ -107,10 +115,6 @@
     while len(terms) > 1:
         terms = [a + b for a, b in zip(terms[::2], terms[1::2])]
     out[...] = terms[0]
-
-
-def spread(ref, row):
-    return jnp.transpose(jnp.broadcast_to(ref[row : row + 1, :], (TOKENS, HEAD)))
 
 
 def load_lines(pair):
@@ -381,7 +385,7 @@
         hidden_kernel,
         jax.ShapeDtypeStruct((2 * beams, HEAD), BF16),
         (core,),
-        ((ids // vocab_rows)[:, None], *looked),
+        ((ids // vocab_rows).reshape(-1, HEAD), *looked),
         "hidden",
     )
     hidden = [hidden] + [cross(hidden, "x", k) for k in (1, 2, 3)]
@@ -396,7 +400,7 @@
         project_kernel,
         jax.ShapeDtypeStruct((16, TILES, HEAD), F32),
         (),
-        (parent.reshape(-1, 1), beam_id.reshape(1, -1), *hidden, *weights),
+        (parent.reshape(1, -1), beam_id.reshape(1, -1), *hidden, *weights),
         "project",
         scratch=[
             pltpu.VMEM((2 * beams, q_cols + HEAD), F32),
@@ -424,13 +428,12 @@
     carry = attend(((0, 0, 0), (2, 0, 1)), (), near + far, "attend_near")
     carry, part = lax.optimization_barrier((carry, part))
     part = call(sum_kernel, jax.ShapeDtypeStruct((TILES, HEAD), F32), (), (part,), "sum")
-    sides = []
-    for i in range(2):
-        pairs = []
-        for at in range(64):
-            h, j, p, l, c = at >> 4, (at >> 3) & 1, (at >> 2) & 1, (at >> 1) & 1, at & 1
-            pairs.append((at, (((2 * j + c) * 4 + h) * 2 + l) * 2 + (p ^ i)))
-        sides.append(lax.ppermute(part, ("zh", "x", "zl", "c"), pairs))
+    pairs = []
+    for at in range(64):
+        h, j, p, l, c = at >> 4, (at >> 3) & 1, (at >> 2) & 1, (at >> 1) & 1, at & 1
+        pairs.append((at, (((2 * j + c) * 4 + h) * 2 + l) * 2 + p))
+    mine = lax.ppermute(part, ("zh", "x", "zl", "c"), pairs)
+    sides = (mine, lax.ppermute(mine, "c", [(0, 1), (1, 0)]))
     keep, send = attend(
         ((4, 0, 2), (4, 1, 3)),
         carry,

time: 145 us -> 149 us (1.028)
  waiting for transfers between devices: 21.2 us -> 26.4 us
  starting transfers between devices: 48.8 us -> 46.5 us
    all_to_all x1, waiting for transfers between devices: 2.24 us -> 11.5 us  [shards(): lax.all_to_all(packed, DEPTH, split_axis=0, concat_axis=0, tiled=True)]
    all_to_all x1, starting transfers between devices: 7.9 us -> 3.61 us  [shards(): lax.all_to_all(part, ('zh', 'y'), split_axis=0, concat_axis=0, tiled=True)]
    all_to_all x1, waiting for transfers between devices: 3.37 us -> 0.01 us  [shards(): lax.all_to_all(part, ('zh', 'y'), split_axis=0, concat_axis=0, tiled=True)]
    ppermute x1, starting transfers between devices: 1.64 us -> 4.31 us  [shards(): packed_other = lax.ppermute(packed, 'c', [(0, 1), (1, 0)])]
    all_to_all x1, starting transfers between devices: 9.01 us -> 6.56 us  [shards(): lax.all_to_all(packed, DEPTH, split_axis=0, concat_axis=0, tiled=True)]
    ppermute x9, starting transfers between devices: 12.6 us -> 14.5 us  [cross(): return lax.ppermute(v, axis, [(i, i ^ k) for i in range(4)])]
  transfers between devices with their start and end apart: 24 -> 24, of which waited for: 13 -> 11; matrix products, arithmetic and copies ran while one was open for 7% -> 4% of each run, Pallas kernels for 12% -> 13%
where the time goes in v1:
time: 149 us; the launch traced here: 148 us
  starting transfers between devices  46.5 us (31%)
  Pallas kernels  36.8 us (25%)
  waiting for transfers between devices  26.4 us (18%)
  blocking collectives  23.2 us (16%)
  local copies, waits for them, and re-layouts  11.1 us (7%)
  other arithmetic  3.13 us (2%)
    pallas_call x8, Pallas kernels, call(): pl.pallas_call(kernel, out_shape=out_shape, in_specs=[SMEM_SPEC] * len(sc...  36.8 us
    all_to_all x1, blocking collectives, shards(): lax.all_to_all(messages, 'zh', split_axis=0, concat_axis=0, tiled=True)  23.2 us
    ppermute x9, starting transfers between devices, cross(): return lax.ppermute(v, axis, [(i, i ^ k) for i in range(4)])  14.5 us
    all_to_all x1, waiting for transfers between devices, shards(): lax.all_to_all(packed, DEPTH, split_axis=0, concat_axis=0, tiled=True)  11.5 us
    ppermute x8, starting transfers between devices, swap(): return lax.ppermute(v, (axis, 'c'), pairs)  9.1 us
    all_to_all x1, starting transfers between devices, shards(): lax.all_to_all(packed, DEPTH, split_axis=0, concat_axis=0, tiled=True)  6.56 us
    ppermute x1, starting transfers between devices, shards(): mine = lax.ppermute(part, ('zh', 'x', 'zl', 'c'), pairs)  5.87 us
    ppermute x8, waiting for transfers between devices, swap(): return lax.ppermute(v, (axis, 'c'), pairs)  4.72 us
  transfers between devices with their start and end apart: 24, of which 11 were waited for; matrix products, arithmetic and copies ran while one was open for 4% of the time, Pallas kernels for 13%

profile of v1, /device:TPU:1, one launch (start us, length us, event | category | flops | bytes accessed | tf_op | source)
XLA Modules:
  0.0 148.2 jit_solution(14197357956026492903)
XLA Ops:
  0.6 0.8 reshape.101
  2.0 3.5 %gather_fusion = bf16[256,128]{1,0:T(8,128)(2,1)S(1)} fusion(bf16[16384,128]{1,0:T(8,128)(2,1)} %param.19, s32[1024]{0:T(1024)S(1)} %pad_clamp_fusion), kind=kCustom, calls=%fused_computation | custom fusion | bytes 132096 | tf_op jit(solution)/shard_map/gather | solution.py:344
  5.4 3.1 %collective-permute-start.8 = (bf16[256,128]{1,0:T(8,128)(2,1)S(1)}, bf16[256,128]{1,0:T(8,128)(2,1)S(1)}, u32[]{:S(2)}, u32[]{:S(2)}) collective-permute-start(bf16[256,128]{1,0:T(8,128)(2,1)S(1)} %gather_fusion), channel_id=1, source_target_pairs={{0,3},{1,2},{2,1},{3,0},{4,7},{5,6},{6,5},{7,4},{8,11},{9,10},{10,... | collective-permute-start | bytes 196616 | tf_op jit(solution)/shard_map/ppermute | solution.py:337
  8.5 1.6 %collective-permute-start.7 = (bf16[256,128]{1,0:T(8,128)(2,1)S(1)}, bf16[256,128]{1,0:T(8,128)(2,1)S(1)}, u32[]{:S(2)}, u32[]{:S(2)}) collective-permute-start(bf16[256,128]{1,0:T(8,128)(2,1)S(1)} %gather_fusion), channel_id=1, source_target_pairs={{0,2},{1,3},{2,0},{3,1},{4,6},{5,7},{6,4},{7,5},{8,10},{9,11},{10,... | collective-permute-start | bytes 196616 | tf_op jit(solution)/shard_map/ppermute | solution.py:337
  10.1 0.6 pad_add_fusion.1.core.refs_0_
  10.7 2.3 %pack.1 = (bf16[8,112,256]{2,1,0:T(8,128)(2,1)}, bf16[128,640]{1,0:T(8,128)(2,1)}, bf16[128,640]{1,0:T(8,128)(2,1)}, bf16[128,640]{1,0:T(8,128)(2,1)}, bf16[128,640]{1,0:T(8,128)(2,1)}) custom-call(s32[4]{0:T(128)} %pad_add_fusion.1.core.refs_0_, bf16[32,1024]{1,0:T(8,128)(2,1)} %old_k.1, bf16[32,1024]{1,0:T(8,128)(2,1)} %old_v.1, bf16[16,1024]{1,0:T(8,128)(2,1)} %new_k.1, ...), custom_call_target="tpu_custom_call" | custom-call | tf_op jit(solution)/shard_map/pack/pallas_call | solution.py:40
  13.1 6.6 %all-to-all-start = ((bf16[8,112,256]{2,1,0:T(8,128)(2,1)}), bf16[8,112,256]{2,1,0:T(8,128)(2,1)S(1)}, u32[]{:S(2)}, u32[]{:S(2)}) async-start(bf16[8,112,256]{2,1,0:T(8,128)(2,1)} %get-tuple-element.37), calls=%async_computation | async-start | bytes 917504 | tf_op jit(solution)/shard_map/all_to_all | solution.py:334
  19.6 1.2 collective-permute-start.3
  20.8 2.5 %collective-permute-start.4 = (bf16[128,640]{1,0:T(8,128)(2,1)}, bf16[128,640]{1,0:T(8,128)(2,1)S(1)}, u32[]{:S(2)}, u32[]{:S(2)}) collective-permute-start(bf16[128,640]{1,0:T(8,128)(2,1)} %get-tuple-element.40), channel_id=1, source_target_pairs={{0,32},{16,48},{32,0},{48,16},{1,33},{17,49},{33,1},{49,17},{2,34}... | collective-permute-start | bytes 491528 | tf_op jit(solution)/shard_map/ppermute | solution.py:337
  23.3 0.9 reshape.97
  24.7 11.5 %all-to-all-done.refs_3_ = bf16[8,112,256]{2,1,0:T(8,128)(2,1)S(1)} async-done(((bf16[8,112,256]{2,1,0:T(8,128)(2,1)}), bf16[8,112,256]{2,1,0:T(8,128)(2,1)S(1)}, u32[]{:S(2)}, u32[]{:S(2)}) %all-to-all-start) | async-done | bytes 458784 | tf_op jit(solution)/shard_map/all_to_all | solution.py:334
  36.2 2.6 %collective-permute-start.5 = (bf16[128,640]{1,0:T(8,128)(2,1)}, bf16[128,640]{1,0:T(8,128)(2,1)S(1)}, u32[]{:S(2)}, u32[]{:S(2)}) collective-permute-start(bf16[128,640]{1,0:T(8,128)(2,1)} %get-tuple-element.41), channel_id=1, source_target_pairs={{0,48},{16,32},{32,16},{48,0},{1,49},{17,33},{33,17},{49,1},{2,50}... | collective-permute-start | bytes 491528 | tf_op jit(solution)/shard_map/ppermute | solution.py:337
  38.8 2.7 %collective-permute-start.2 = (bf16[1,4,48,256]{3,2,1,0:T(8,128)(2,1)S(1)}, bf16[1,4,48,256]{3,2,1,0:T(8,128)(2,1)S(1)}, u32[]{:S(2)}, u32[]{:S(2)}) collective-permute-start(bf16[1,4,48,256]{3,2,1,0:T(8,128)(2,1)S(1)} %get-tuple-element.72), channel_id=1, source_target_pairs={{0,4},{1,13},{4,0},{5,9},{8,12},{9,5},{12,8},{13,1},{2,6},{3,15},{... | collective-permute-start | bytes 294920 | tf_op jit(solution)/shard_map/ppermute | solution.py:353
  42.3 0.7 collective-permute-done.5.refs_7_
  43.0 0.8 collective-permute-done.2
  43.8 2.4 %collective-permute-done.1 = bf16[1,4,48,256]{3,2,1,0:T(8,128)(2,1)S(1)} collective-permute-done((bf16[1,4,48,256]{3,2,1,0:T(8,128)(2,1)S(1)}, bf16[1,4,48,256]{3,2,1,0:T(8,128)(2,1)S(1)}, u32[]{:S(2)}, u32[]{:S(2)}) %collective-permute-start.1) | collective-permute-done | bytes 98336 | tf_op jit(solution)/shard_map/ppermute | solution.py:353
  46.5 1.7 %hidden.1.refs_0_ = bf16[256,128]{1,0:T(8,128)(2,1)} custom-call(s32[4]{0:T(128)} %pad_add_fusion.1.core.refs_0_, s32[2,128]{1,0:T(2,128)} %and_select_fusion.1.owner, bf16[256,128]{1,0:T(8,128)(2,1)} %copy-done.9, bf16[256,128]{1,0:T(8,128)(2,1)} %copy-done.15, bf16[256,128]{1,0:T(8,128)(2,1)} %copy-done.14, bf16[256,128]{1,0:T(8,128)(2,1)} %copy-done.13), custom_call_target="tpu_custom_call" | custom-call | tf_op jit(solution)/shard_map/hidden/pallas_call | solution.py:40
  48.2 2.4 %collective-permute-start.13 = (bf16[256,128]{1,0:T(8,128)(2,1)}, bf16[256,128]{1,0:T(8,128)(2,1)S(1)}, u32[]{:S(2)}, u32[]{:S(2)}) collective-permute-start(bf16[256,128]{1,0:T(8,128)(2,1)} %hidden.1.refs_0_), channel_id=1, source_target_pairs={{0,48},{16,32},{32,16},{48,0},{1,49},{17,33},{33,17},{49,1},{2,50}... | collective-permute-start | bytes 196616 | tf_op jit(solution)/shard_map/ppermute | solution.py:337
  50.7 1.2 collective-permute-start.12
  52.0 1.3 collective-permute-done.13.refs_3_
  53.3 2.3 %collective-permute-done.12.refs_2_ = bf16[256,128]{1,0:T(8,128)(2,1)S(1)} collective-permute-done((bf16[256,128]{1,0:T(8,128)(2,1)}, bf16[256,128]{1,0:T(8,128)(2,1)S(1)}, u32[]{:S(2)}, u32[]{:S(2)}) %collective-permute-start.12) | collective-permute-done | bytes 65568 | tf_op jit(solution)/shard_map/ppermute | solution.py:337
  55.6 1.9 %collective-permute-start.15 = (bf16[4,4,48,256]{3,2,1,0:T(8,128)(2,1)S(1)}, bf16[4,4,48,256]{3,2,1,0:T(8,128)(2,1)S(1)}, u32[]{:S(2)}, u32[]{:S(2)}) collective-permute-start(bf16[4,4,48,256]{3,2,1,0:T(8,128)(2,1)S(1)} %pad_maximum_fusion.3.refs_6_.refs_10_), channel_id=1, source_target_pairs={{0,16},{1,49},{16,0},{17,33},{32,48},{33,17},{48,32},{49,1},{2,18}... | collective-permute-start | bytes 1179656 | tf_op jit(solution)/shard_map/ppermute | solution.py:353
  57.5 2.1 %collective-permute-start.14 = (bf16[4,4,48,256]{3,2,1,0:T(8,128)(2,1)S(1)}, bf16[4,4,48,256]{3,2,1,0:T(8,128)(2,1)S(1)}, u32[]{:S(2)}, u32[]{:S(2)}) collective-permute-start(bf16[4,4,48,256]{3,2,1,0:T(8,128)(2,1)S(1)} %pad_maximum_fusion.2.refs_5_.refs_9_), channel_id=1, source_target_pairs={{0,4},{1,13},{4,0},{5,9},{8,12},{9,5},{12,8},{13,1},{2,6},{3,15},{... | collective-permute-start | bytes 1179656 | tf_op jit(solution)/shard_map/ppermute | solution.py:353
  60.0 0.6 reshape.105.parent
  60.7 3.1 %project.1 = f32[16,88,128]{2,1,0:T(8,128)} custom-call(s32[1,128]{1,0:T(1,128)} %reshape.105.parent, s32[1,128]{1,0:T(1,128)} %constant.87.clone.beam_id, bf16[256,128]{1,0:T(8,128)(2,1)} %hidden.1.refs_0_, bf16[256,128]{1,0:T(8,128)(2,1)} %copy-done.18, bf16[256,128]{1,0:T(8,128)(2,1)} %copy-done.17, bf16[256,128]{1,0:T(8,128)(2,1)} %copy-done.16, ...), custom_call_target="tpu_custom_call" | custom-call | tf_op jit(solution)/shard_map/project/pallas_call | solution.py:40
  63.9 1.5 %collective-permute-done.14.refs_7_.refs_11_ = bf16[4,4,48,256]{3,2,1,0:T(8,128)(2,1)S(1)} collective-permute-done((bf16[4,4,48,256]{3,2,1,0:T(8,128)(2,1)S(1)}, bf16[4,4,48,256]{3,2,1,0:T(8,128)(2,1)S(1)}, u32[]{:S(2)}, u32[]{:S(2)}) %collective-permute-start.14) | collective-permute-done | bytes 393248 | tf_op jit(solution)/shard_map/ppermute | solution.py:353
  65.4 1.0 pad_maximum_fusion
  66.4 3.6 %all-to-all-start.1 = ((f32[16,88,128]{2,1,0:T(8,128)}), f32[16,88,128]{2,1,0:T(8,128)S(1)}, u32[]{:S(2)}, u32[]{:S(2)}) async-start(f32[16,88,128]{2,1,0:T(8,128)} %project.1), calls=%async_computation.1 | async-start | bytes 1441792 | tf_op jit(solution)/shard_map/all_to_all | solution.py:412
  70.0 4.3 %collective-permute-start = (bf16[8,112,256]{2,1,0:T(8,128)(2,1)S(1)}, bf16[8,112,256]{2,1,0:T(8,128)(2,1)}, u32[]{:S(2)}, u32[]{:S(2)}) collective-permute-start(bf16[8,112,256]{2,1,0:T(8,128)(2,1)S(1)} %all-to-all-done.refs_3_), channel_id=1, source_target_pairs={{0,1},{1,0},{2,3},{3,2},{4,5},{5,4},{6,7},{7,6},{8,9},{9,8},{10,11... | collective-permute-start | bytes 1376264 | tf_op jit(solution)/shard_map/ppermute | solution.py:362
  74.3 0.8 reshape.98.refs_1_
  75.4 1.5 %collective-permute-start.18 = (bf16[8,4,48,256]{3,2,1,0:T(8,128)(2,1)}, bf16[8,4,48,256]{3,2,1,0:T(8,128)(2,1)}, u32[]{:S(2)}, u32[]{:S(2)}) collective-permute-start(bf16[8,4,48,256]{3,2,1,0:T(8,128)(2,1)} %pad_maximum_fusion), channel_id=1, source_target_pairs={{0,12},{1,5},{4,8},{5,1},{8,4},{9,13},{12,0},{13,9},{2,14},{3,7},{... | collective-permute-start | bytes 2359304 | tf_op jit(solution)/shard_map/ppermute | solution.py:353
  77.3 0.6 pad_add_fusion.refs_2_
  77.9 10.6 %attend_near.1 = (f32[1056,128]{1,0:T(8,128)}, f32[1056,128]{1,0:T(8,128)}) custom-call(s32[4]{0:T(128)} %pad_add_fusion.1.core.refs_0_, s32[32,128]{1,0:T(8,128)} %reshape.98.refs_1_, s32[8,256]{1,0:T(8,128)} %pad_add_fusion.refs_2_, bf16[8,112,256]{2,1,0:T(8,128)(2,1)} %copy-done.4, bf16[8,112,256]{2,1,0:T(8,128)(2,1)} %collective-permute-done.refs_4_, ...), custom_call_target="tpu_custom_call" | custom-call | flops 6442450944 | bytes 1572864 | tf_op jit(solution)/shard_map/attend_near/pallas_call | solution.py:40
  88.5 0.8 copy-done
  89.4 1.8 %sum.1 = f32[88,128]{1,0:T(8,128)} custom-call(f32[16,88,128]{2,1,0:T(8,128)} %copy-done), custom_call_target="tpu_custom_call" | custom-call | tf_op jit(solution)/shard_map/sum/pallas_call | solution.py:40
  91.2 5.9 %collective-permute-start.16 = (f32[88,128]{1,0:T(8,128)}, f32[88,128]{1,0:T(8,128)S(1)}, u32[]{:S(2)}, u32[]{:S(2)}) collective-permute-start(f32[88,128]{1,0:T(8,128)} %sum.1), channel_id=1, source_target_pairs={{0,0},{1,64},{2,2},{3,66},{16,1},{17,65},{18,3},{19,67},{32,128},{... | collective-permute-start | bytes 135176 | tf_op jit(solution)/shard_map/ppermute | solution.py:435
  97.0 1.4 collective-permute-done.16.refs_5_
  98.5 1.2 collective-permute-done.17.refs_6_
  99.7 0.6 copy-done.21
  100.3 12.9 %attend_rest.1 = (f32[1184,128]{1,0:T(8,128)}, f32[1184,128]{1,0:T(8,128)}) custom-call(s32[4]{0:T(128)} %pad_add_fusion.1.core.refs_0_, s32[32,128]{1,0:T(8,128)} %reshape.98.refs_1_, s32[8,256]{1,0:T(8,128)} %pad_add_fusion.refs_2_, bf16[8,112,256]{2,1,0:T(8,128)(2,1)} %copy-done.4, bf16[8,112,256]{2,1,0:T(8,128)(2,1)} %collective-permute-done.refs_4_, ...), custom_call_target="tpu_custom_call" | custom-call | flops 6442450944 | bytes 1572864 | tf_op jit(solution)/shard_map/attend_rest/pallas_call | solution.py:40
  113.3 2.1 %collective-permute-done.20.got = f32[1184,128]{1,0:T(8,128)S(1)} collective-permute-done((f32[1184,128]{1,0:T(8,128)}, f32[1184,128]{1,0:T(8,128)S(1)}, u32[]{:S(2)}, u32[]{:S(2)}) %collective-permute-start.20) | collective-permute-done | bytes 606240 | tf_op jit(solution)/shard_map/ppermute | solution.py:445
  115.4 0.8 copy-done.5
  116.2 2.7 %merge.1 = bf16[4,32,1152]{2,1,0:T(8,128)(2,1)} custom-call(s32[4]{0:T(128)} %pad_add_fusion.1.core.refs_0_, f32[1184,128]{1,0:T(8,128)} %get-tuple-element.70.keep, f32[1184,128]{1,0:T(8,128)} %copy-done.5), custom_call_target="tpu_custom_call" | custom-call | tf_op jit(solution)/shard_map/merge/pallas_call | solution.py:40
  118.9 23.2 %all_to_all.15.near = bf16[4,32,1152]{2,1,0:T(8,128)(2,1)S(1)} all-to-all(bf16[4,32,1152]{2,1,0:T(8,128)(2,1)} %merge.1), channel_id=1, replica_groups=mesh['zh'=4,'x'=4,'y'=4,'zl'=2,'c'=2] {'zh'}, dimensions={0} | all-to-all | bytes 589824 | tf_op jit(solution)/shard_map/all_to_all | solution.py:455
  142.1 2.4 %collective-permute-start.21 = (bf16[4,32,1152]{2,1,0:T(8,128)(2,1)S(1)}, bf16[4,32,1152]{2,1,0:T(8,128)(2,1)S(1)}, u32[]{:S(2)}, u32[]{:S(2)}) collective-permute-start(bf16[4,32,1152]{2,1,0:T(8,128)(2,1)S(1)} %all_to_all.15.near), channel_id=1, source_target_pairs={{0,1},{1,0},{2,3},{3,2},{4,5},{5,4},{6,7},{7,6},{8,9},{9,8},{10,11... | collective-permute-start | bytes 884744 | tf_op jit(solution)/shard_map/ppermute | solution.py:456
  144.5 1.2 collective-permute-done.21.far
  145.7 0.7 copy-done.8
  146.4 1.8 %place.1 = (bf16[64,2048]{1,0:T(8,128)(2,1)}, bf16[2,2,2048]{2,1,0:T(2,128)(2,1)}) custom-call(s32[4]{0:T(128)} %pad_add_fusion.1.core.refs_0_, bf16[4,32,1152]{2,1,0:T(8,128)(2,1)} %copy-done.3, bf16[4,32,1152]{2,1,0:T(8,128)(2,1)} %copy-done.8), custom_call_target="tpu_custom_call" | custom-call | tf_op jit(solution)/shard_map/place/pallas_call | solution.py:40
  (94 shorter events, 3.4 us)
Async XLA Ops:
  0.6 59.0 %copy-start.19 = (s32[128]{0:T(128)S(1)}, s32[128]{0:T(128)}, u32[]{:S(2)}) copy-start(s32[128]{0:T(128)} %param.24) | copy-start | bytes 1540
  5.4 41.1 %copy-start.9 = (bf16[256,128]{1,0:T(8,128)(2,1)}, bf16[256,128]{1,0:T(8,128)(2,1)S(1)}, u32[]{:S(2)}) copy-start(bf16[256,128]{1,0:T(8,128)(2,1)S(1)} %gather_fusion) | copy-start | bytes 196612
  5.4 30.8 %collective-permute-start.8 = (bf16[256,128]{1,0:T(8,128)(2,1)S(1)}, bf16[256,128]{1,0:T(8,128)(2,1)S(1)}, u32[]{:S(2)}, u32[]{:S(2)}) collective-permute-start(bf16[256,128]{1,0:T(8,128)(2,1)S(1)} %gather_fusion), channel_id=1, source_target_pairs={{0,3},{1,2},{2,1},{3,0},{4,7},{5,6},{6,5},{7,4},{8,11},{9,10},{10,... | collective-permute-start | bytes 196616 | tf_op jit(solution)/shard_map/ppermute | solution.py:337
  8.5 30.2 %collective-permute-start.7 = (bf16[256,128]{1,0:T(8,128)(2,1)S(1)}, bf16[256,128]{1,0:T(8,128)(2,1)S(1)}, u32[]{:S(2)}, u32[]{:S(2)}) collective-permute-start(bf16[256,128]{1,0:T(8,128)(2,1)S(1)} %gather_fusion), channel_id=1, source_target_pairs={{0,2},{1,3},{2,0},{3,1},{4,6},{5,7},{6,4},{7,5},{8,10},{9,11},{10,... | collective-permute-start | bytes 196616 | tf_op jit(solution)/shard_map/ppermute | solution.py:337
  10.1 31.4 %collective-permute-start.6 = (bf16[256,128]{1,0:T(8,128)(2,1)S(1)}, bf16[256,128]{1,0:T(8,128)(2,1)S(1)}, u32[]{:S(2)}, u32[]{:S(2)}) collective-permute-start(bf16[256,128]{1,0:T(8,128)(2,1)S(1)} %gather_fusion), channel_id=1, source_target_pairs={{0,1},{1,0},{2,3},{3,2},{4,5},{5,4},{6,7},{7,6},{8,9},{9,8},{10,11... | collective-permute-start | bytes 196616 | tf_op jit(solution)/shard_map/ppermute | solution.py:337
  13.1 23.1 %all-to-all-start = ((bf16[8,112,256]{2,1,0:T(8,128)(2,1)}), bf16[8,112,256]{2,1,0:T(8,128)(2,1)S(1)}, u32[]{:S(2)}, u32[]{:S(2)}) async-start(bf16[8,112,256]{2,1,0:T(8,128)(2,1)} %get-tuple-element.37), calls=%async_computation | async-start | bytes 917504 | tf_op jit(solution)/shard_map/all_to_all | solution.py:334
  19.6 22.7 %collective-permute-start.3 = (bf16[128,640]{1,0:T(8,128)(2,1)}, bf16[128,640]{1,0:T(8,128)(2,1)S(1)}, u32[]{:S(2)}, u32[]{:S(2)}) collective-permute-start(bf16[128,640]{1,0:T(8,128)(2,1)} %get-tuple-element.39), channel_id=1, source_target_pairs={{0,16},{16,0},{32,48},{48,32},{1,17},{17,1},{33,49},{49,33},{2,18}... | collective-permute-start | bytes 491528 | tf_op jit(solution)/shard_map/ppermute | solution.py:337
  20.8 21.5 %collective-permute-start.4 = (bf16[128,640]{1,0:T(8,128)(2,1)}, bf16[128,640]{1,0:T(8,128)(2,1)S(1)}, u32[]{:S(2)}, u32[]{:S(2)}) collective-permute-start(bf16[128,640]{1,0:T(8,128)(2,1)} %get-tuple-element.40), channel_id=1, source_target_pairs={{0,32},{16,48},{32,0},{48,16},{1,33},{17,49},{33,1},{49,17},{2,34}... | collective-permute-start | bytes 491528 | tf_op jit(solution)/shard_map/ppermute | solution.py:337
  36.2 33.8 %copy-start.4 = (bf16[8,112,256]{2,1,0:T(8,128)(2,1)}, bf16[8,112,256]{2,1,0:T(8,128)(2,1)S(1)}, u32[]{:S(2)}) copy-start(bf16[8,112,256]{2,1,0:T(8,128)(2,1)S(1)} %all-to-all-done.refs_3_) | copy-start | bytes 1376260
  36.2 10.3 %copy-start.13 = (bf16[256,128]{1,0:T(8,128)(2,1)}, bf16[256,128]{1,0:T(8,128)(2,1)S(1)}, u32[]{:S(2)}) copy-start(bf16[256,128]{1,0:T(8,128)(2,1)S(1)} %collective-permute-done.8.refs_3_) | copy-start | bytes 196612
  36.2 6.8 %collective-permute-start.5 = (bf16[128,640]{1,0:T(8,128)(2,1)}, bf16[128,640]{1,0:T(8,128)(2,1)S(1)}, u32[]{:S(2)}, u32[]{:S(2)}) collective-permute-start(bf16[128,640]{1,0:T(8,128)(2,1)} %get-tuple-element.41), channel_id=1, source_target_pairs={{0,48},{16,32},{32,16},{48,0},{1,49},{17,33},{33,17},{49,1},{2,50}... | collective-permute-start | bytes 491528 | tf_op jit(solution)/shard_map/ppermute | solution.py:337
  38.8 7.7 %copy-start.14 = (bf16[256,128]{1,0:T(8,128)(2,1)}, bf16[256,128]{1,0:T(8,128)(2,1)S(1)}, u32[]{:S(2)}) copy-start(bf16[256,128]{1,0:T(8,128)(2,1)S(1)} %collective-permute-done.7.refs_2_) | copy-start | bytes 196612
  38.8 5.0 %collective-permute-start.2 = (bf16[1,4,48,256]{3,2,1,0:T(8,128)(2,1)S(1)}, bf16[1,4,48,256]{3,2,1,0:T(8,128)(2,1)S(1)}, u32[]{:S(2)}, u32[]{:S(2)}) collective-permute-start(bf16[1,4,48,256]{3,2,1,0:T(8,128)(2,1)S(1)} %get-tuple-element.72), channel_id=1, source_target_pairs={{0,4},{1,13},{4,0},{5,9},{8,12},{9,5},{12,8},{13,1},{2,6},{3,15},{... | collective-permute-start | bytes 294920 | tf_op jit(solution)/shard_map/ppermute | solution.py:353
  41.5 5.0 %copy-start.15 = (bf16[256,128]{1,0:T(8,128)(2,1)}, bf16[256,128]{1,0:T(8,128)(2,1)S(1)}, u32[]{:S(2)}) copy-start(bf16[256,128]{1,0:T(8,128)(2,1)S(1)} %collective-permute-done.6.refs_1_) | copy-start | bytes 196612
  41.5 4.7 %collective-permute-start.1 = (bf16[1,4,48,256]{3,2,1,0:T(8,128)(2,1)S(1)}, bf16[1,4,48,256]{3,2,1,0:T(8,128)(2,1)S(1)}, u32[]{:S(2)}, u32[]{:S(2)}) collective-permute-start(bf16[1,4,48,256]{3,2,1,0:T(8,128)(2,1)S(1)} %get-tuple-element.73), channel_id=1, source_target_pairs={{0,16},{1,49},{16,0},{17,33},{32,48},{33,17},{48,32},{49,1},{2,18}... | collective-permute-start | bytes 294920 | tf_op jit(solution)/shard_map/ppermute | solution.py:353
  42.3 18.4 %copy-start.10 = (bf16[128,640]{1,0:T(8,128)(2,1)}, bf16[128,640]{1,0:T(8,128)(2,1)S(1)}, u32[]{:S(2)}) copy-start(bf16[128,640]{1,0:T(8,128)(2,1)S(1)} %collective-permute-done.3.refs_5_) | copy-start | bytes 491524
  42.3 18.4 %copy-start.11 = (bf16[128,640]{1,0:T(8,128)(2,1)}, bf16[128,640]{1,0:T(8,128)(2,1)S(1)}, u32[]{:S(2)}) copy-start(bf16[128,640]{1,0:T(8,128)(2,1)S(1)} %collective-permute-done.4.refs_6_) | copy-start | bytes 491524
  43.0 17.7 %copy-start.12 = (bf16[128,640]{1,0:T(8,128)(2,1)}, bf16[128,640]{1,0:T(8,128)(2,1)S(1)}, u32[]{:S(2)}) copy-start(bf16[128,640]{1,0:T(8,128)(2,1)S(1)} %collective-permute-done.5.refs_7_) | copy-start | bytes 491524
  46.2 5.6 %collective-permute-start.10 = (bf16[2,4,48,256]{3,2,1,0:T(8,128)(2,1)S(1)}, bf16[2,4,48,256]{3,2,1,0:T(8,128)(2,1)S(1)}, u32[]{:S(2)}, u32[]{:S(2)}) collective-permute-start(bf16[2,4,48,256]{3,2,1,0:T(8,128)(2,1)S(1)} %pad_maximum_fusion.5), channel_id=1, source_target_pairs={{0,12},{1,5},{4,8},{5,1},{8,4},{9,13},{12,0},{13,9},{2,14},{3,7},{... | collective-permute-start | bytes 589832 | tf_op jit(solution)/shard_map/ppermute | solution.py:353
  46.4 5.5 %collective-permute-start.9 = (bf16[2,4,48,256]{3,2,1,0:T(8,128)(2,1)S(1)}, bf16[2,4,48,256]{3,2,1,0:T(8,128)(2,1)S(1)}, u32[]{:S(2)}, u32[]{:S(2)}) collective-permute-start(bf16[2,4,48,256]{3,2,1,0:T(8,128)(2,1)S(1)} %pad_maximum_fusion.4), channel_id=1, source_target_pairs={{0,48},{1,17},{16,32},{17,1},{32,16},{33,49},{48,0},{49,33},{2,50}... | collective-permute-start | bytes 589832 | tf_op jit(solution)/shard_map/ppermute | solution.py:353
  48.2 5.1 %collective-permute-start.13 = (bf16[256,128]{1,0:T(8,128)(2,1)}, bf16[256,128]{1,0:T(8,128)(2,1)S(1)}, u32[]{:S(2)}, u32[]{:S(2)}) collective-permute-start(bf16[256,128]{1,0:T(8,128)(2,1)} %hidden.1.refs_0_), channel_id=1, source_target_pairs={{0,48},{16,32},{32,16},{48,0},{1,49},{17,33},{33,17},{49,1},{2,50}... | collective-permute-start | bytes 196616 | tf_op jit(solution)/shard_map/ppermute | solution.py:337
  50.7 4.9 %collective-permute-start.12 = (bf16[256,128]{1,0:T(8,128)(2,1)}, bf16[256,128]{1,0:T(8,128)(2,1)S(1)}, u32[]{:S(2)}, u32[]{:S(2)}) collective-permute-start(bf16[256,128]{1,0:T(8,128)(2,1)} %hidden.1.refs_0_), channel_id=1, source_target_pairs={{0,32},{16,48},{32,0},{48,16},{1,33},{17,49},{33,1},{49,17},{2,34}... | collective-permute-start | bytes 196616 | tf_op jit(solution)/shard_map/ppermute | solution.py:337
  51.8 3.8 %collective-permute-start.11 = (bf16[256,128]{1,0:T(8,128)(2,1)}, bf16[256,128]{1,0:T(8,128)(2,1)S(1)}, u32[]{:S(2)}, u32[]{:S(2)}) collective-permute-start(bf16[256,128]{1,0:T(8,128)(2,1)} %hidden.1.refs_0_), channel_id=1, source_target_pairs={{0,16},{16,0},{32,48},{48,32},{1,17},{17,1},{33,49},{49,33},{2,18}... | collective-permute-start | bytes 196616 | tf_op jit(solution)/shard_map/ppermute | solution.py:337
  51.9 26.0 %copy-start.1 = (bf16[4,4,48,256]{3,2,1,0:T(8,128)(2,1)}, bf16[4,4,48,256]{3,2,1,0:T(8,128)(2,1)S(1)}, u32[]{:S(2)}) copy-start(bf16[4,4,48,256]{3,2,1,0:T(8,128)(2,1)S(1)} %pad_maximum_fusion.3.refs_6_.refs_10_) | copy-start | bytes 1179652
  51.9 26.0 %copy-start.2 = (bf16[4,4,48,256]{3,2,1,0:T(8,128)(2,1)}, bf16[4,4,48,256]{3,2,1,0:T(8,128)(2,1)S(1)}, u32[]{:S(2)}) copy-start(bf16[4,4,48,256]{3,2,1,0:T(8,128)(2,1)S(1)} %pad_maximum_fusion.2.refs_5_.refs_9_) | copy-start | bytes 1179652
  53.3 7.4 %copy-start.16 = (bf16[256,128]{1,0:T(8,128)(2,1)}, bf16[256,128]{1,0:T(8,128)(2,1)S(1)}, u32[]{:S(2)}) copy-start(bf16[256,128]{1,0:T(8,128)(2,1)S(1)} %collective-permute-done.13.refs_3_) | copy-start | bytes 196612
  55.6 5.1 %copy-start.17 = (bf16[256,128]{1,0:T(8,128)(2,1)}, bf16[256,128]{1,0:T(8,128)(2,1)S(1)}, u32[]{:S(2)}) copy-start(bf16[256,128]{1,0:T(8,128)(2,1)S(1)} %collective-permute-done.12.refs_2_) | copy-start | bytes 196612
  55.6 5.1 %copy-start.18 = (bf16[256,128]{1,0:T(8,128)(2,1)}, bf16[256,128]{1,0:T(8,128)(2,1)S(1)}, u32[]{:S(2)}) copy-start(bf16[256,128]{1,0:T(8,128)(2,1)S(1)} %collective-permute-done.11.refs_1_) | copy-start | bytes 196612
  55.6 8.2 %collective-permute-start.15 = (bf16[4,4,48,256]{3,2,1,0:T(8,128)(2,1)S(1)}, bf16[4,4,48,256]{3,2,1,0:T(8,128)(2,1)S(1)}, u32[]{:S(2)}, u32[]{:S(2)}) collective-permute-start(bf16[4,4,48,256]{3,2,1,0:T(8,128)(2,1)S(1)} %pad_maximum_fusion.3.refs_6_.refs_10_), channel_id=1, source_target_pairs={{0,16},{1,49},{16,0},{17,33},{32,48},{33,17},{48,32},{49,1},{2,18}... | collective-permute-start | bytes 1179656 | tf_op jit(solution)/shard_map/ppermute | solution.py:353
  57.5 7.8 %collective-permute-start.14 = (bf16[4,4,48,256]{3,2,1,0:T(8,128)(2,1)S(1)}, bf16[4,4,48,256]{3,2,1,0:T(8,128)(2,1)S(1)}, u32[]{:S(2)}, u32[]{:S(2)}) collective-permute-start(bf16[4,4,48,256]{3,2,1,0:T(8,128)(2,1)S(1)} %pad_maximum_fusion.2.refs_5_.refs_9_), channel_id=1, source_target_pairs={{0,4},{1,13},{4,0},{5,9},{8,12},{9,5},{12,8},{13,1},{2,6},{3,15},{... | collective-permute-start | bytes 1179656 | tf_op jit(solution)/shard_map/ppermute | solution.py:353
  63.8 14.2 %copy-start.6 = (bf16[4,4,48,256]{3,2,1,0:T(8,128)(2,1)}, bf16[4,4,48,256]{3,2,1,0:T(8,128)(2,1)S(1)}, u32[]{:S(2)}) copy-start(bf16[4,4,48,256]{3,2,1,0:T(8,128)(2,1)S(1)} %collective-permute-done.15.refs_8_.refs_12_) | copy-start | bytes 1179652
  65.4 1.0 copy-start.7
  66.4 22.2 %all-to-all-start.1 = ((f32[16,88,128]{2,1,0:T(8,128)}), f32[16,88,128]{2,1,0:T(8,128)S(1)}, u32[]{:S(2)}, u32[]{:S(2)}) async-start(f32[16,88,128]{2,1,0:T(8,128)} %project.1), calls=%async_computation.1 | async-start | bytes 1441792 | tf_op jit(solution)/shard_map/all_to_all | solution.py:412
  70.0 7.9 %collective-permute-start = (bf16[8,112,256]{2,1,0:T(8,128)(2,1)S(1)}, bf16[8,112,256]{2,1,0:T(8,128)(2,1)}, u32[]{:S(2)}, u32[]{:S(2)}) collective-permute-start(bf16[8,112,256]{2,1,0:T(8,128)(2,1)S(1)} %all-to-all-done.refs_3_), channel_id=1, source_target_pairs={{0,1},{1,0},{2,3},{3,2},{4,5},{5,4},{6,7},{7,6},{8,9},{9,8},{10,11... | collective-permute-start | bytes 1376264 | tf_op jit(solution)/shard_map/ppermute | solution.py:362
  75.4 23.1 %collective-permute-start.18 = (bf16[8,4,48,256]{3,2,1,0:T(8,128)(2,1)}, bf16[8,4,48,256]{3,2,1,0:T(8,128)(2,1)}, u32[]{:S(2)}, u32[]{:S(2)}) collective-permute-start(bf16[8,4,48,256]{3,2,1,0:T(8,128)(2,1)} %pad_maximum_fusion), channel_id=1, source_target_pairs={{0,12},{1,5},{4,8},{5,1},{8,4},{9,13},{12,0},{13,9},{2,14},{3,7},{... | collective-permute-start | bytes 2359304 | tf_op jit(solution)/shard_map/ppermute | solution.py:353
  76.9 21.6 %collective-permute-start.19 = (bf16[8,4,48,256]{3,2,1,0:T(8,128)(2,1)S(1)}, bf16[8,4,48,256]{3,2,1,0:T(8,128)(2,1)}, u32[]{:S(2)}, u32[]{:S(2)}) collective-permute-start(bf16[8,4,48,256]{3,2,1,0:T(8,128)(2,1)S(1)} %pad_maximum_fusion.1), channel_id=1, source_target_pairs={{0,48},{1,17},{16,32},{17,1},{32,16},{33,49},{48,0},{49,33},{2,50}... | collective-permute-start | bytes 2359304 | tf_op jit(solution)/shard_map/ppermute | solution.py:353
  88.5 0.8 copy-start
  91.2 7.3 %collective-permute-start.16 = (f32[88,128]{1,0:T(8,128)}, f32[88,128]{1,0:T(8,128)S(1)}, u32[]{:S(2)}, u32[]{:S(2)}) collective-permute-start(f32[88,128]{1,0:T(8,128)} %sum.1), channel_id=1, source_target_pairs={{0,0},{1,64},{2,2},{3,66},{16,1},{17,65},{18,3},{19,67},{32,128},{... | collective-permute-start | bytes 135176 | tf_op jit(solution)/shard_map/ppermute | solution.py:435
  98.5 1.2 copy-start.20
  98.5 1.2 collective-permute-start.17
  99.7 0.6 copy-start.21
  113.2 2.2 %collective-permute-start.20 = (f32[1184,128]{1,0:T(8,128)}, f32[1184,128]{1,0:T(8,128)S(1)}, u32[]{:S(2)}, u32[]{:S(2)}) collective-permute-start(f32[1184,128]{1,0:T(8,128)} %get-tuple-element.71), channel_id=1, source_target_pairs={{0,1},{1,0},{2,3},{3,2},{4,5},{5,4},{6,7},{7,6},{8,9},{9,8},{10,11... | collective-permute-start | bytes 1818632 | tf_op jit(solution)/shard_map/ppermute | solution.py:445
  115.4 0.8 copy-start.5
  142.1 3.6 %copy-start.3 = (bf16[4,32,1152]{2,1,0:T(8,128)(2,1)}, bf16[4,32,1152]{2,1,0:T(8,128)(2,1)S(1)}, u32[]{:S(2)}) copy-start(bf16[4,32,1152]{2,1,0:T(8,128)(2,1)S(1)} %all_to_all.15.near) | copy-start | bytes 884740
  142.1 3.6 %collective-permute-start.21 = (bf16[4,32,1152]{2,1,0:T(8,128)(2,1)S(1)}, bf16[4,32,1152]{2,1,0:T(8,128)(2,1)S(1)}, u32[]{:S(2)}, u32[]{:S(2)}) collective-permute-start(bf16[4,32,1152]{2,1,0:T(8,128)(2,1)S(1)} %all_to_all.15.near), channel_id=1, source_target_pairs={{0,1},{1,0},{2,3},{3,2},{4,5},{5,4},{6,7},{7,6},{8,9},{9,8},{10,11... | collective-permute-start | bytes 884744 | tf_op jit(solution)/shard_map/ppermute | solution.py:456
  145.7 0.7 copy-start.8

commit v2 on v1

--- a/solution.py
+++ b/solution.py
@@ -425,7 +425,7 @@
             ),
         )
 
-    carry = attend(((0, 0, 0), (2, 0, 1)), (), near + far, "attend_near")
+    carry = attend(((0, 0, 0),), (), near, "attend_near")
     carry, part = lax.optimization_barrier((carry, part))
     part = call(sum_kernel, jax.ShapeDtypeStruct((TILES, HEAD), F32), (), (part,), "sum")
     pairs = []
@@ -434,6 +434,7 @@
         pairs.append((at, (((2 * j + c) * 4 + h) * 2 + l) * 2 + p))
     mine = lax.ppermute(part, ("zh", "x", "zl", "c"), pairs)
     sides = (mine, lax.ppermute(mine, "c", [(0, 1), (1, 0)]))
+    carry = attend(((0, 0, 1),), carry, far, "attend_far")
     keep, send = attend(
         ((4, 0, 2), (4, 1, 3)),
         carry,

time: 149 us -> 150 us (level)
  Pallas kernels: 36.8 us -> 40.1 us
  blocking collectives: 23.2 us -> 20.4 us
    all_to_all x1, waiting for transfers between devices: 11.5 us -> 3.01 us  [shards(): lax.all_to_all(packed, DEPTH, split_axis=0, concat_axis=0, tiled=True)]
    all_to_all x1, waiting for transfers between devices: 0.01 us -> 7.77 us  [shards(): lax.all_to_all(part, ('zh', 'y'), split_axis=0, concat_axis=0, tiled=True)]
    all_to_all x1, starting transfers between devices: 3.61 us -> 7.16 us  [shards(): lax.all_to_all(part, ('zh', 'y'), split_axis=0, concat_axis=0, tiled=True)]
    pallas_call x8 -> x9, Pallas kernels: 36.8 us -> 40.1 us  [call(): pl.pallas_call(kernel, out_shape=out_shape, in_specs=[SMEM_SPEC] * len(sc...]
    all_to_all x1, blocking collectives: 23.2 us -> 20.4 us  [shards(): lax.all_to_all(messages, 'zh', split_axis=0, concat_axis=0, tiled=True)]
    ppermute x1, starting transfers between devices: 4.31 us -> 1.81 us  [shards(): packed_other = lax.ppermute(packed, 'c', [(0, 1), (1, 0)])]
    all_to_all x1, starting transfers between devices: 6.56 us -> 9.01 us  [shards(): lax.all_to_all(packed, DEPTH, split_axis=0, concat_axis=0, tiled=True)]
    ppermute x9, starting transfers between devices: 14.5 us -> 12.6 us  [cross(): return lax.ppermute(v, axis, [(i, i ^ k) for i in range(4)])]
  transfers between devices with their start and end apart: 24 -> 24, of which waited for: 11 -> 13; matrix products, arithmetic and copies ran while one was open for 4% -> 6% of each run, Pallas kernels for 13% -> 14%
where the time goes in v2:
time: 150 us; the launch traced here: 149 us
  starting transfers between devices  47.9 us (32%)
  Pallas kernels  40.1 us (27%)
  waiting for transfers between devices  25.4 us (17%)
  blocking collectives  20.4 us (14%)
  local copies, waits for them, and re-layouts  11.2 us (7%)
  other arithmetic  3.14 us (2%)
    pallas_call x9, Pallas kernels, call(): pl.pallas_call(kernel, out_shape=out_shape, in_specs=[SMEM_SPEC] * len(sc...  40.1 us
    all_to_all x1, blocking collectives, shards(): lax.all_to_all(messages, 'zh', split_axis=0, concat_axis=0, tiled=True)  20.4 us
    ppermute x9, starting transfers between devices, cross(): return lax.ppermute(v, axis, [(i, i ^ k) for i in range(4)])  12.6 us
    ppermute x8, starting transfers between devices, swap(): return lax.ppermute(v, (axis, 'c'), pairs)  9.59 us
    all_to_all x1, starting transfers between devices, shards(): lax.all_to_all(packed, DEPTH, split_axis=0, concat_axis=0, tiled=True)  9.01 us
    all_to_all x1, waiting for transfers between devices, shards(): lax.all_to_all(part, ('zh', 'y'), split_axis=0, concat_axis=0, tiled=True)  7.77 us
    all_to_all x1, starting transfers between devices, shards(): lax.all_to_all(part, ('zh', 'y'), split_axis=0, concat_axis=0, tiled=True)  7.16 us
    ppermute x8, waiting for transfers between devices, swap(): return lax.ppermute(v, (axis, 'c'), pairs)  5.95 us
  transfers between devices with their start and end apart: 24, of which 13 were waited for; matrix products, arithmetic and copies ran while one was open for 6% of the time, Pallas kernels for 14%

profile of v2, /device:TPU:1, one launch (start us, length us, event | category | flops | bytes accessed | tf_op | source)
XLA Modules:
  0.0 149.1 jit_solution(17503596850081444561)
XLA Ops:
  0.7 0.6 pad_add_fusion.1.core.refs_0_
  1.3 2.3 %pack.1 = (bf16[8,112,256]{2,1,0:T(8,128)(2,1)}, bf16[128,640]{1,0:T(8,128)(2,1)}, bf16[128,640]{1,0:T(8,128)(2,1)}, bf16[128,640]{1,0:T(8,128)(2,1)}, bf16[128,640]{1,0:T(8,128)(2,1)}) custom-call(s32[4]{0:T(128)} %pad_add_fusion.1.core.refs_0_, bf16[32,1024]{1,0:T(8,128)(2,1)} %old_k.1, bf16[32,1024]{1,0:T(8,128)(2,1)} %old_v.1, bf16[16,1024]{1,0:T(8,128)(2,1)} %new_k.1, ...), custom_call_target="tpu_custom_call" | custom-call | tf_op jit(solution)/shard_map/pack/pallas_call | solution.py:40
  3.6 9.0 %all-to-all-start = ((bf16[8,112,256]{2,1,0:T(8,128)(2,1)}), bf16[8,112,256]{2,1,0:T(8,128)(2,1)S(1)}, u32[]{:S(2)}, u32[]{:S(2)}) async-start(bf16[8,112,256]{2,1,0:T(8,128)(2,1)} %get-tuple-element.39), calls=%async_computation | async-start | bytes 917504 | tf_op jit(solution)/shard_map/all_to_all | solution.py:334
  12.6 0.8 reshape.101
  13.9 3.5 %gather_fusion = bf16[256,128]{1,0:T(8,128)(2,1)S(1)} fusion(bf16[16384,128]{1,0:T(8,128)(2,1)} %param.19, s32[1024]{0:T(1024)S(1)} %pad_clamp_fusion), kind=kCustom, calls=%fused_computation | custom fusion | bytes 132096 | tf_op jit(solution)/shard_map/gather | solution.py:344
  17.4 2.7 %collective-permute-start.8 = (bf16[256,128]{1,0:T(8,128)(2,1)S(1)}, bf16[256,128]{1,0:T(8,128)(2,1)S(1)}, u32[]{:S(2)}, u32[]{:S(2)}) collective-permute-start(bf16[256,128]{1,0:T(8,128)(2,1)S(1)} %gather_fusion), channel_id=1, source_target_pairs={{0,3},{1,2},{2,1},{3,0},{4,7},{5,6},{6,5},{7,4},{8,11},{9,10},{10,... | collective-permute-start | bytes 196616 | tf_op jit(solution)/shard_map/ppermute | solution.py:337
  20.5 1.2 collective-permute-start.3
  21.7 2.5 %collective-permute-start.4 = (bf16[128,640]{1,0:T(8,128)(2,1)}, bf16[128,640]{1,0:T(8,128)(2,1)S(1)}, u32[]{:S(2)}, u32[]{:S(2)}) collective-permute-start(bf16[128,640]{1,0:T(8,128)(2,1)} %get-tuple-element.42), channel_id=1, source_target_pairs={{0,32},{16,48},{32,0},{48,16},{1,33},{17,49},{33,1},{49,17},{2,34}... | collective-permute-start | bytes 491528 | tf_op jit(solution)/shard_map/ppermute | solution.py:337
  24.2 0.9 reshape.97
  25.4 3.0 %all-to-all-done.refs_3_ = bf16[8,112,256]{2,1,0:T(8,128)(2,1)S(1)} async-done(((bf16[8,112,256]{2,1,0:T(8,128)(2,1)}), bf16[8,112,256]{2,1,0:T(8,128)(2,1)S(1)}, u32[]{:S(2)}, u32[]{:S(2)}) %all-to-all-start) | async-done | bytes 458784 | tf_op jit(solution)/shard_map/all_to_all | solution.py:334
  28.5 2.6 %collective-permute-start.5 = (bf16[128,640]{1,0:T(8,128)(2,1)}, bf16[128,640]{1,0:T(8,128)(2,1)S(1)}, u32[]{:S(2)}, u32[]{:S(2)}) collective-permute-start(bf16[128,640]{1,0:T(8,128)(2,1)} %get-tuple-element.43), channel_id=1, source_target_pairs={{0,48},{16,32},{32,16},{48,0},{1,49},{17,33},{33,17},{49,1},{2,50}... | collective-permute-start | bytes 491528 | tf_op jit(solution)/shard_map/ppermute | solution.py:337
  31.1 2.7 %collective-permute-start.2 = (bf16[1,4,48,256]{3,2,1,0:T(8,128)(2,1)S(1)}, bf16[1,4,48,256]{3,2,1,0:T(8,128)(2,1)S(1)}, u32[]{:S(2)}, u32[]{:S(2)}) collective-permute-start(bf16[1,4,48,256]{3,2,1,0:T(8,128)(2,1)S(1)} %get-tuple-element.76), channel_id=1, source_target_pairs={{0,4},{1,13},{4,0},{5,9},{8,12},{9,5},{12,8},{13,1},{2,6},{3,15},{... | collective-permute-start | bytes 294920 | tf_op jit(solution)/shard_map/ppermute | solution.py:353
  34.5 1.6 %collective-permute-done.2 = bf16[1,4,48,256]{3,2,1,0:T(8,128)(2,1)S(1)} collective-permute-done((bf16[1,4,48,256]{3,2,1,0:T(8,128)(2,1)S(1)}, bf16[1,4,48,256]{3,2,1,0:T(8,128)(2,1)S(1)}, u32[]{:S(2)}, u32[]{:S(2)}) %collective-permute-start.2) | collective-permute-done | bytes 98336 | tf_op jit(solution)/shard_map/ppermute | solution.py:353
  36.1 2.4 %collective-permute-done.1 = bf16[1,4,48,256]{3,2,1,0:T(8,128)(2,1)S(1)} collective-permute-done((bf16[1,4,48,256]{3,2,1,0:T(8,128)(2,1)S(1)}, bf16[1,4,48,256]{3,2,1,0:T(8,128)(2,1)S(1)}, u32[]{:S(2)}, u32[]{:S(2)}) %collective-permute-start.1) | collective-permute-done | bytes 98336 | tf_op jit(solution)/shard_map/ppermute | solution.py:353
  39.3 1.7 %hidden.1.refs_0_ = bf16[256,128]{1,0:T(8,128)(2,1)} custom-call(s32[4]{0:T(128)} %pad_add_fusion.1.core.refs_0_, s32[2,128]{1,0:T(2,128)} %and_select_fusion.1.owner, bf16[256,128]{1,0:T(8,128)(2,1)} %copy-done.9, bf16[256,128]{1,0:T(8,128)(2,1)} %copy-done.15, bf16[256,128]{1,0:T(8,128)(2,1)} %copy-done.14, bf16[256,128]{1,0:T(8,128)(2,1)} %copy-done.13), custom_call_target="tpu_custom_call" | custom-call | tf_op jit(solution)/shard_map/hidden/pallas_call | solution.py:40
  41.0 1.8 %collective-permute-start.13 = (bf16[256,128]{1,0:T(8,128)(2,1)}, bf16[256,128]{1,0:T(8,128)(2,1)S(1)}, u32[]{:S(2)}, u32[]{:S(2)}) collective-permute-start(bf16[256,128]{1,0:T(8,128)(2,1)} %hidden.1.refs_0_), channel_id=1, source_target_pairs={{0,48},{16,32},{32,16},{48,0},{1,49},{17,33},{33,17},{49,1},{2,50}... | collective-permute-start | bytes 196616 | tf_op jit(solution)/shard_map/ppermute | solution.py:337
  42.9 1.4 collective-permute-start.12
  44.4 1.9 %collective-permute-done.13.refs_3_ = bf16[256,128]{1,0:T(8,128)(2,1)S(1)} collective-permute-done((bf16[256,128]{1,0:T(8,128)(2,1)}, bf16[256,128]{1,0:T(8,128)(2,1)S(1)}, u32[]{:S(2)}, u32[]{:S(2)}) %collective-permute-start.13) | collective-permute-done | bytes 65568 | tf_op jit(solution)/shard_map/ppermute | solution.py:337
  46.3 1.5 collective-permute-done.12.refs_2_
  47.9 1.8 %collective-permute-start.15 = (bf16[4,4,48,256]{3,2,1,0:T(8,128)(2,1)S(1)}, bf16[4,4,48,256]{3,2,1,0:T(8,128)(2,1)S(1)}, u32[]{:S(2)}, u32[]{:S(2)}) collective-permute-start(bf16[4,4,48,256]{3,2,1,0:T(8,128)(2,1)S(1)} %pad_maximum_fusion.3.refs_6_.refs_10_), channel_id=1, source_target_pairs={{0,16},{1,49},{16,0},{17,33},{32,48},{33,17},{48,32},{49,1},{2,18}... | collective-permute-start | bytes 1179656 | tf_op jit(solution)/shard_map/ppermute | solution.py:353
  49.8 1.7 %collective-permute-start.14 = (bf16[4,4,48,256]{3,2,1,0:T(8,128)(2,1)S(1)}, bf16[4,4,48,256]{3,2,1,0:T(8,128)(2,1)S(1)}, u32[]{:S(2)}, u32[]{:S(2)}) collective-permute-start(bf16[4,4,48,256]{3,2,1,0:T(8,128)(2,1)S(1)} %pad_maximum_fusion.2.refs_5_.refs_9_), channel_id=1, source_target_pairs={{0,4},{1,13},{4,0},{5,9},{8,12},{9,5},{12,8},{13,1},{2,6},{3,15},{... | collective-permute-start | bytes 1179656 | tf_op jit(solution)/shard_map/ppermute | solution.py:353
  51.9 0.6 reshape.105.parent
  52.5 3.1 %project.1 = f32[16,88,128]{2,1,0:T(8,128)} custom-call(s32[1,128]{1,0:T(1,128)} %reshape.105.parent, s32[1,128]{1,0:T(1,128)} %constant.87.clone.beam_id, bf16[256,128]{1,0:T(8,128)(2,1)} %hidden.1.refs_0_, bf16[256,128]{1,0:T(8,128)(2,1)} %copy-done.18, bf16[256,128]{1,0:T(8,128)(2,1)} %copy-done.17, bf16[256,128]{1,0:T(8,128)(2,1)} %copy-done.16, ...), custom_call_target="tpu_custom_call" | custom-call | tf_op jit(solution)/shard_map/project/pallas_call | solution.py:40
  56.1 1.5 %collective-permute-done.14.refs_7_.refs_11_ = bf16[4,4,48,256]{3,2,1,0:T(8,128)(2,1)S(1)} collective-permute-done((bf16[4,4,48,256]{3,2,1,0:T(8,128)(2,1)S(1)}, bf16[4,4,48,256]{3,2,1,0:T(8,128)(2,1)S(1)}, u32[]{:S(2)}, u32[]{:S(2)}) %collective-permute-start.14) | collective-permute-done | bytes 393248 | tf_op jit(solution)/shard_map/ppermute | solution.py:353
  57.7 1.0 pad_maximum_fusion
  58.7 7.2 %all-to-all-start.1 = ((f32[16,88,128]{2,1,0:T(8,128)}), f32[16,88,128]{2,1,0:T(8,128)S(1)}, u32[]{:S(2)}, u32[]{:S(2)}) async-start(f32[16,88,128]{2,1,0:T(8,128)} %project.1), calls=%async_computation.1 | async-start | bytes 1441792 | tf_op jit(solution)/shard_map/all_to_all | solution.py:412
  66.0 1.8 %collective-permute-start = (bf16[8,112,256]{2,1,0:T(8,128)(2,1)S(1)}, bf16[8,112,256]{2,1,0:T(8,128)(2,1)}, u32[]{:S(2)}, u32[]{:S(2)}) collective-permute-start(bf16[8,112,256]{2,1,0:T(8,128)(2,1)S(1)} %all-to-all-done.refs_3_), channel_id=1, source_target_pairs={{0,1},{1,0},{2,3},{3,2},{4,5},{5,4},{6,7},{7,6},{8,9},{9,8},{10,11... | collective-permute-start | bytes 1376264 | tf_op jit(solution)/shard_map/ppermute | solution.py:362
  67.8 1.7 %collective-permute-start.18 = (bf16[8,4,48,256]{3,2,1,0:T(8,128)(2,1)}, bf16[8,4,48,256]{3,2,1,0:T(8,128)(2,1)}, u32[]{:S(2)}, u32[]{:S(2)}) collective-permute-start(bf16[8,4,48,256]{3,2,1,0:T(8,128)(2,1)} %pad_maximum_fusion), channel_id=1, source_target_pairs={{0,12},{1,5},{4,8},{5,1},{8,4},{9,13},{12,0},{13,9},{2,14},{3,7},{... | collective-permute-start | bytes 2359304 | tf_op jit(solution)/shard_map/ppermute | solution.py:353
  69.5 1.2 collective-permute-start.19
  70.8 0.8 reshape.98.refs_1_
  71.8 0.6 pad_add_fusion.refs_2_
  72.4 6.4 %attend_near.1 = (f32[1056,128]{1,0:T(8,128)}, f32[1056,128]{1,0:T(8,128)}) custom-call(s32[4]{0:T(128)} %pad_add_fusion.1.core.refs_0_, s32[32,128]{1,0:T(8,128)} %reshape.98.refs_1_, s32[8,256]{1,0:T(8,128)} %pad_add_fusion.refs_2_, bf16[8,112,256]{2,1,0:T(8,128)(2,1)} %copy-done.4, bf16[8,112,256]{2,1,0:T(8,128)(2,1)} %collective-permute-done.refs_4_, ...), custom_call_target="tpu_custom_call" | custom-call | flops 3221225472 | bytes 786432 | tf_op jit(solution)/shard_map/attend_near/pallas_call | solution.py:40
  78.8 7.8 %all-to-all-done.1.parts = f32[16,88,128]{2,1,0:T(8,128)S(1)} async-done(((f32[16,88,128]{2,1,0:T(8,128)}), f32[16,88,128]{2,1,0:T(8,128)S(1)}, u32[]{:S(2)}, u32[]{:S(2)}) %all-to-all-start.1) | async-done | bytes 720928 | tf_op jit(solution)/shard_map/all_to_all | solution.py:412
  86.6 0.9 copy-done
  87.5 1.8 %sum.1 = f32[88,128]{1,0:T(8,128)} custom-call(f32[16,88,128]{2,1,0:T(8,128)} %copy-done), custom_call_target="tpu_custom_call" | custom-call | tf_op jit(solution)/shard_map/sum/pallas_call | solution.py:40
  89.2 5.0 %collective-permute-start.16 = (f32[88,128]{1,0:T(8,128)}, f32[88,128]{1,0:T(8,128)S(1)}, u32[]{:S(2)}, u32[]{:S(2)}) collective-permute-start(f32[88,128]{1,0:T(8,128)} %sum.1), channel_id=1, source_target_pairs={{0,0},{1,64},{2,2},{3,66},{16,1},{17,65},{18,3},{19,67},{32,128},{... | collective-permute-start | bytes 135176 | tf_op jit(solution)/shard_map/ppermute | solution.py:435
  94.3 1.7 %collective-permute-done.16.refs_5_ = f32[88,128]{1,0:T(8,128)S(1)} collective-permute-done((f32[88,128]{1,0:T(8,128)}, f32[88,128]{1,0:T(8,128)S(1)}, u32[]{:S(2)}, u32[]{:S(2)}) %collective-permute-start.16) | collective-permute-done | bytes 45088 | tf_op jit(solution)/shard_map/ppermute | solution.py:435
  96.0 7.2 %attend_far.1 = (f32[1056,128]{1,0:T(8,128)}, f32[1056,128]{1,0:T(8,128)}) custom-call(s32[4]{0:T(128)} %pad_add_fusion.1.core.refs_0_, s32[32,128]{1,0:T(8,128)} %reshape.98.refs_1_, s32[8,256]{1,0:T(8,128)} %pad_add_fusion.refs_2_, bf16[8,112,256]{2,1,0:T(8,128)(2,1)} %copy-done.4, bf16[8,112,256]{2,1,0:T(8,128)(2,1)} %collective-permute-done.refs_4_, ...), custom_call_target="tpu_custom_call" | custom-call | flops 3221225472 | bytes 786432 | tf_op jit(solution)/shard_map/attend_far/pallas_call | solution.py:40
  103.2 0.6 copy-done.21
  103.8 13.2 %attend_rest.1 = (f32[1184,128]{1,0:T(8,128)}, f32[1184,128]{1,0:T(8,128)}) custom-call(s32[4]{0:T(128)} %pad_add_fusion.1.core.refs_0_, s32[32,128]{1,0:T(8,128)} %reshape.98.refs_1_, s32[8,256]{1,0:T(8,128)} %pad_add_fusion.refs_2_, bf16[8,112,256]{2,1,0:T(8,128)(2,1)} %copy-done.4, bf16[8,112,256]{2,1,0:T(8,128)(2,1)} %collective-permute-done.refs_4_, ...), custom_call_target="tpu_custom_call" | custom-call | flops 6442450944 | bytes 1572864 | tf_op jit(solution)/shard_map/attend_rest/pallas_call | solution.py:40
  117.4 1.9 %collective-permute-done.20.got = f32[1184,128]{1,0:T(8,128)S(1)} collective-permute-done((f32[1184,128]{1,0:T(8,128)}, f32[1184,128]{1,0:T(8,128)S(1)}, u32[]{:S(2)}, u32[]{:S(2)}) %collective-permute-start.20) | collective-permute-done | bytes 606240 | tf_op jit(solution)/shard_map/ppermute | solution.py:446
  119.3 0.8 copy-done.5
  120.1 2.7 %merge.1 = bf16[4,32,1152]{2,1,0:T(8,128)(2,1)} custom-call(s32[4]{0:T(128)} %pad_add_fusion.1.core.refs_0_, f32[1184,128]{1,0:T(8,128)} %get-tuple-element.74.keep, f32[1184,128]{1,0:T(8,128)} %copy-done.5), custom_call_target="tpu_custom_call" | custom-call | tf_op jit(solution)/shard_map/merge/pallas_call | solution.py:40
  122.8 20.4 %all_to_all.15.near = bf16[4,32,1152]{2,1,0:T(8,128)(2,1)S(1)} all-to-all(bf16[4,32,1152]{2,1,0:T(8,128)(2,1)} %merge.1), channel_id=1, replica_groups=mesh['zh'=4,'x'=4,'y'=4,'zl'=2,'c'=2] {'zh'}, dimensions={0} | all-to-all | bytes 589824 | tf_op jit(solution)/shard_map/all_to_all | solution.py:456
  143.2 2.2 %collective-permute-start.21 = (bf16[4,32,1152]{2,1,0:T(8,128)(2,1)S(1)}, bf16[4,32,1152]{2,1,0:T(8,128)(2,1)S(1)}, u32[]{:S(2)}, u32[]{:S(2)}) collective-permute-start(bf16[4,32,1152]{2,1,0:T(8,128)(2,1)S(1)} %all_to_all.15.near), channel_id=1, source_target_pairs={{0,1},{1,0},{2,3},{3,2},{4,5},{5,4},{6,7},{7,6},{8,9},{9,8},{10,11... | collective-permute-start | bytes 884744 | tf_op jit(solution)/shard_map/ppermute | solution.py:457
  145.4 1.2 collective-permute-done.21.far
  146.6 0.7 copy-done.8
  147.3 1.8 %place.1 = (bf16[64,2048]{1,0:T(8,128)(2,1)}, bf16[2,2,2048]{2,1,0:T(2,128)(2,1)}) custom-call(s32[4]{0:T(128)} %pad_add_fusion.1.core.refs_0_, bf16[4,32,1152]{2,1,0:T(8,128)(2,1)} %copy-done.3, bf16[4,32,1152]{2,1,0:T(8,128)(2,1)} %copy-done.8), custom_call_target="tpu_custom_call" | custom-call | tf_op jit(solution)/shard_map/place/pallas_call | solution.py:40
  (95 shorter events, 4.7 us)
Async XLA Ops:
  0.6 50.9 %copy-start.19 = (s32[128]{0:T(128)S(1)}, s32[128]{0:T(128)}, u32[]{:S(2)}) copy-start(s32[128]{0:T(128)} %param.24) | copy-start | bytes 1540
  3.6 24.9 %all-to-all-start = ((bf16[8,112,256]{2,1,0:T(8,128)(2,1)}), bf16[8,112,256]{2,1,0:T(8,128)(2,1)S(1)}, u32[]{:S(2)}, u32[]{:S(2)}) async-start(bf16[8,112,256]{2,1,0:T(8,128)(2,1)} %get-tuple-element.39), calls=%async_computation | async-start | bytes 917504 | tf_op jit(solution)/shard_map/all_to_all | solution.py:334
  17.4 22.0 %copy-start.9 = (bf16[256,128]{1,0:T(8,128)(2,1)}, bf16[256,128]{1,0:T(8,128)(2,1)S(1)}, u32[]{:S(2)}) copy-start(bf16[256,128]{1,0:T(8,128)(2,1)S(1)} %gather_fusion) | copy-start | bytes 196612
  17.4 11.1 %collective-permute-start.8 = (bf16[256,128]{1,0:T(8,128)(2,1)S(1)}, bf16[256,128]{1,0:T(8,128)(2,1)S(1)}, u32[]{:S(2)}, u32[]{:S(2)}) collective-permute-start(bf16[256,128]{1,0:T(8,128)(2,1)S(1)} %gather_fusion), channel_id=1, source_target_pairs={{0,3},{1,2},{2,1},{3,0},{4,7},{5,6},{6,5},{7,4},{8,11},{9,10},{10,... | collective-permute-start | bytes 196616 | tf_op jit(solution)/shard_map/ppermute | solution.py:337
  20.0 11.0 %collective-permute-start.7 = (bf16[256,128]{1,0:T(8,128)(2,1)S(1)}, bf16[256,128]{1,0:T(8,128)(2,1)S(1)}, u32[]{:S(2)}, u32[]{:S(2)}) collective-permute-start(bf16[256,128]{1,0:T(8,128)(2,1)S(1)} %gather_fusion), channel_id=1, source_target_pairs={{0,2},{1,3},{2,0},{3,1},{4,6},{5,7},{6,4},{7,5},{8,10},{9,11},{10,... | collective-permute-start | bytes 196616 | tf_op jit(solution)/shard_map/ppermute | solution.py:337
  20.0 13.8 %collective-permute-start.6 = (bf16[256,128]{1,0:T(8,128)(2,1)S(1)}, bf16[256,128]{1,0:T(8,128)(2,1)S(1)}, u32[]{:S(2)}, u32[]{:S(2)}) collective-permute-start(bf16[256,128]{1,0:T(8,128)(2,1)S(1)} %gather_fusion), channel_id=1, source_target_pairs={{0,1},{1,0},{2,3},{3,2},{4,5},{5,4},{6,7},{7,6},{8,9},{9,8},{10,11... | collective-permute-start | bytes 196616 | tf_op jit(solution)/shard_map/ppermute | solution.py:337
  20.5 13.6 %collective-permute-start.3 = (bf16[128,640]{1,0:T(8,128)(2,1)}, bf16[128,640]{1,0:T(8,128)(2,1)S(1)}, u32[]{:S(2)}, u32[]{:S(2)}) collective-permute-start(bf16[128,640]{1,0:T(8,128)(2,1)} %get-tuple-element.41), channel_id=1, source_target_pairs={{0,16},{16,0},{32,48},{48,32},{1,17},{17,1},{33,49},{49,33},{2,18}... | collective-permute-start | bytes 491528 | tf_op jit(solution)/shard_map/ppermute | solution.py:337
  21.7 12.4 %collective-permute-start.4 = (bf16[128,640]{1,0:T(8,128)(2,1)}, bf16[128,640]{1,0:T(8,128)(2,1)S(1)}, u32[]{:S(2)}, u32[]{:S(2)}) collective-permute-start(bf16[128,640]{1,0:T(8,128)(2,1)} %get-tuple-element.42), channel_id=1, source_target_pairs={{0,32},{16,48},{32,0},{48,16},{1,33},{17,49},{33,1},{49,17},{2,34}... | collective-permute-start | bytes 491528 | tf_op jit(solution)/shard_map/ppermute | solution.py:337
  28.5 37.5 %copy-start.4 = (bf16[8,112,256]{2,1,0:T(8,128)(2,1)}, bf16[8,112,256]{2,1,0:T(8,128)(2,1)S(1)}, u32[]{:S(2)}) copy-start(bf16[8,112,256]{2,1,0:T(8,128)(2,1)S(1)} %all-to-all-done.refs_3_) | copy-start | bytes 1376260
  28.5 10.8 %copy-start.13 = (bf16[256,128]{1,0:T(8,128)(2,1)}, bf16[256,128]{1,0:T(8,128)(2,1)S(1)}, u32[]{:S(2)}) copy-start(bf16[256,128]{1,0:T(8,128)(2,1)S(1)} %collective-permute-done.8.refs_3_) | copy-start | bytes 196612
  28.5 6.0 %collective-permute-start.5 = (bf16[128,640]{1,0:T(8,128)(2,1)}, bf16[128,640]{1,0:T(8,128)(2,1)S(1)}, u32[]{:S(2)}, u32[]{:S(2)}) collective-permute-start(bf16[128,640]{1,0:T(8,128)(2,1)} %get-tuple-element.43), channel_id=1, source_target_pairs={{0,48},{16,32},{32,16},{48,0},{1,49},{17,33},{33,17},{49,1},{2,50}... | collective-permute-start | bytes 491528 | tf_op jit(solution)/shard_map/ppermute | solution.py:337
  31.1 8.3 %copy-start.14 = (bf16[256,128]{1,0:T(8,128)(2,1)}, bf16[256,128]{1,0:T(8,128)(2,1)S(1)}, u32[]{:S(2)}) copy-start(bf16[256,128]{1,0:T(8,128)(2,1)S(1)} %collective-permute-done.7.refs_2_) | copy-start | bytes 196612
  31.1 5.0 %collective-permute-start.2 = (bf16[1,4,48,256]{3,2,1,0:T(8,128)(2,1)S(1)}, bf16[1,4,48,256]{3,2,1,0:T(8,128)(2,1)S(1)}, u32[]{:S(2)}, u32[]{:S(2)}) collective-permute-start(bf16[1,4,48,256]{3,2,1,0:T(8,128)(2,1)S(1)} %get-tuple-element.76), channel_id=1, source_target_pairs={{0,4},{1,13},{4,0},{5,9},{8,12},{9,5},{12,8},{13,1},{2,6},{3,15},{... | collective-permute-start | bytes 294920 | tf_op jit(solution)/shard_map/ppermute | solution.py:353
  33.8 5.5 %copy-start.15 = (bf16[256,128]{1,0:T(8,128)(2,1)}, bf16[256,128]{1,0:T(8,128)(2,1)S(1)}, u32[]{:S(2)}) copy-start(bf16[256,128]{1,0:T(8,128)(2,1)S(1)} %collective-permute-done.6.refs_1_) | copy-start | bytes 196612
  33.8 4.7 %collective-permute-start.1 = (bf16[1,4,48,256]{3,2,1,0:T(8,128)(2,1)S(1)}, bf16[1,4,48,256]{3,2,1,0:T(8,128)(2,1)S(1)}, u32[]{:S(2)}, u32[]{:S(2)}) collective-permute-start(bf16[1,4,48,256]{3,2,1,0:T(8,128)(2,1)S(1)} %get-tuple-element.77), channel_id=1, source_target_pairs={{0,16},{1,49},{16,0},{17,33},{32,48},{33,17},{48,32},{49,1},{2,18}... | collective-permute-start | bytes 294920 | tf_op jit(solution)/shard_map/ppermute | solution.py:353
  34.1 18.4 %copy-start.10 = (bf16[128,640]{1,0:T(8,128)(2,1)}, bf16[128,640]{1,0:T(8,128)(2,1)S(1)}, u32[]{:S(2)}) copy-start(bf16[128,640]{1,0:T(8,128)(2,1)S(1)} %collective-permute-done.3.refs_5_) | copy-start | bytes 491524
  34.2 18.4 %copy-start.11 = (bf16[128,640]{1,0:T(8,128)(2,1)}, bf16[128,640]{1,0:T(8,128)(2,1)S(1)}, u32[]{:S(2)}) copy-start(bf16[128,640]{1,0:T(8,128)(2,1)S(1)} %collective-permute-done.4.refs_6_) | copy-start | bytes 491524
  34.5 18.0 %copy-start.12 = (bf16[128,640]{1,0:T(8,128)(2,1)}, bf16[128,640]{1,0:T(8,128)(2,1)S(1)}, u32[]{:S(2)}) copy-start(bf16[128,640]{1,0:T(8,128)(2,1)S(1)} %collective-permute-done.5.refs_7_) | copy-start | bytes 491524
  38.5 5.8 %collective-permute-start.10 = (bf16[2,4,48,256]{3,2,1,0:T(8,128)(2,1)S(1)}, bf16[2,4,48,256]{3,2,1,0:T(8,128)(2,1)S(1)}, u32[]{:S(2)}, u32[]{:S(2)}) collective-permute-start(bf16[2,4,48,256]{3,2,1,0:T(8,128)(2,1)S(1)} %pad_maximum_fusion.5), channel_id=1, source_target_pairs={{0,12},{1,5},{4,8},{5,1},{8,4},{9,13},{12,0},{13,9},{2,14},{3,7},{... | collective-permute-start | bytes 589832 | tf_op jit(solution)/shard_map/ppermute | solution.py:353
  38.6 5.7 %collective-permute-start.9 = (bf16[2,4,48,256]{3,2,1,0:T(8,128)(2,1)S(1)}, bf16[2,4,48,256]{3,2,1,0:T(8,128)(2,1)S(1)}, u32[]{:S(2)}, u32[]{:S(2)}) collective-permute-start(bf16[2,4,48,256]{3,2,1,0:T(8,128)(2,1)S(1)} %pad_maximum_fusion.4), channel_id=1, source_target_pairs={{0,48},{1,17},{16,32},{17,1},{32,16},{33,49},{48,0},{49,33},{2,50}... | collective-permute-start | bytes 589832 | tf_op jit(solution)/shard_map/ppermute | solution.py:353
  41.0 5.3 %collective-permute-start.13 = (bf16[256,128]{1,0:T(8,128)(2,1)}, bf16[256,128]{1,0:T(8,128)(2,1)S(1)}, u32[]{:S(2)}, u32[]{:S(2)}) collective-permute-start(bf16[256,128]{1,0:T(8,128)(2,1)} %hidden.1.refs_0_), channel_id=1, source_target_pairs={{0,48},{16,32},{32,16},{48,0},{1,49},{17,33},{33,17},{49,1},{2,50}... | collective-permute-start | bytes 196616 | tf_op jit(solution)/shard_map/ppermute | solution.py:337
  42.9 4.9 %collective-permute-start.12 = (bf16[256,128]{1,0:T(8,128)(2,1)}, bf16[256,128]{1,0:T(8,128)(2,1)S(1)}, u32[]{:S(2)}, u32[]{:S(2)}) collective-permute-start(bf16[256,128]{1,0:T(8,128)(2,1)} %hidden.1.refs_0_), channel_id=1, source_target_pairs={{0,32},{16,48},{32,0},{48,16},{1,33},{17,49},{33,1},{49,17},{2,34}... | collective-permute-start | bytes 196616 | tf_op jit(solution)/shard_map/ppermute | solution.py:337
  44.3 3.6 %collective-permute-start.11 = (bf16[256,128]{1,0:T(8,128)(2,1)}, bf16[256,128]{1,0:T(8,128)(2,1)S(1)}, u32[]{:S(2)}, u32[]{:S(2)}) collective-permute-start(bf16[256,128]{1,0:T(8,128)(2,1)} %hidden.1.refs_0_), channel_id=1, source_target_pairs={{0,16},{16,0},{32,48},{48,32},{1,17},{17,1},{33,49},{49,33},{2,18}... | collective-permute-start | bytes 196616 | tf_op jit(solution)/shard_map/ppermute | solution.py:337
  44.4 28.0 %copy-start.1 = (bf16[4,4,48,256]{3,2,1,0:T(8,128)(2,1)}, bf16[4,4,48,256]{3,2,1,0:T(8,128)(2,1)S(1)}, u32[]{:S(2)}) copy-start(bf16[4,4,48,256]{3,2,1,0:T(8,128)(2,1)S(1)} %pad_maximum_fusion.3.refs_6_.refs_10_) | copy-start | bytes 1179652
  44.4 28.0 %copy-start.2 = (bf16[4,4,48,256]{3,2,1,0:T(8,128)(2,1)}, bf16[4,4,48,256]{3,2,1,0:T(8,128)(2,1)S(1)}, u32[]{:S(2)}) copy-start(bf16[4,4,48,256]{3,2,1,0:T(8,128)(2,1)S(1)} %pad_maximum_fusion.2.refs_5_.refs_9_) | copy-start | bytes 1179652
  46.3 6.2 %copy-start.16 = (bf16[256,128]{1,0:T(8,128)(2,1)}, bf16[256,128]{1,0:T(8,128)(2,1)S(1)}, u32[]{:S(2)}) copy-start(bf16[256,128]{1,0:T(8,128)(2,1)S(1)} %collective-permute-done.13.refs_3_) | copy-start | bytes 196612
  47.8 1.9 %copy-start.17 = (bf16[256,128]{1,0:T(8,128)(2,1)}, bf16[256,128]{1,0:T(8,128)(2,1)S(1)}, u32[]{:S(2)}) copy-start(bf16[256,128]{1,0:T(8,128)(2,1)S(1)} %collective-permute-done.12.refs_2_) | copy-start | bytes 196612
  47.9 1.8 %copy-start.18 = (bf16[256,128]{1,0:T(8,128)(2,1)}, bf16[256,128]{1,0:T(8,128)(2,1)S(1)}, u32[]{:S(2)}) copy-start(bf16[256,128]{1,0:T(8,128)(2,1)S(1)} %collective-permute-done.11.refs_1_) | copy-start | bytes 196612
  47.9 8.2 %collective-permute-start.15 = (bf16[4,4,48,256]{3,2,1,0:T(8,128)(2,1)S(1)}, bf16[4,4,48,256]{3,2,1,0:T(8,128)(2,1)S(1)}, u32[]{:S(2)}, u32[]{:S(2)}) collective-permute-start(bf16[4,4,48,256]{3,2,1,0:T(8,128)(2,1)S(1)} %pad_maximum_fusion.3.refs_6_.refs_10_), channel_id=1, source_target_pairs={{0,16},{1,49},{16,0},{17,33},{32,48},{33,17},{48,32},{49,1},{2,18}... | collective-permute-start | bytes 1179656 | tf_op jit(solution)/shard_map/ppermute | solution.py:353
  49.8 7.9 %collective-permute-start.14 = (bf16[4,4,48,256]{3,2,1,0:T(8,128)(2,1)S(1)}, bf16[4,4,48,256]{3,2,1,0:T(8,128)(2,1)S(1)}, u32[]{:S(2)}, u32[]{:S(2)}) collective-permute-start(bf16[4,4,48,256]{3,2,1,0:T(8,128)(2,1)S(1)} %pad_maximum_fusion.2.refs_5_.refs_9_), channel_id=1, source_target_pairs={{0,4},{1,13},{4,0},{5,9},{8,12},{9,5},{12,8},{13,1},{2,6},{3,15},{... | collective-permute-start | bytes 1179656 | tf_op jit(solution)/shard_map/ppermute | solution.py:353
  56.1 22.7 %copy-start.6 = (bf16[4,4,48,256]{3,2,1,0:T(8,128)(2,1)}, bf16[4,4,48,256]{3,2,1,0:T(8,128)(2,1)S(1)}, u32[]{:S(2)}) copy-start(bf16[4,4,48,256]{3,2,1,0:T(8,128)(2,1)S(1)} %collective-permute-done.15.refs_8_.refs_12_) | copy-start | bytes 1179652
  57.7 1.0 copy-start.7
  58.7 27.9 %all-to-all-start.1 = ((f32[16,88,128]{2,1,0:T(8,128)}), f32[16,88,128]{2,1,0:T(8,128)S(1)}, u32[]{:S(2)}, u32[]{:S(2)}) async-start(f32[16,88,128]{2,1,0:T(8,128)} %project.1), calls=%async_computation.1 | async-start | bytes 1441792 | tf_op jit(solution)/shard_map/all_to_all | solution.py:412
  66.0 6.4 %collective-permute-start = (bf16[8,112,256]{2,1,0:T(8,128)(2,1)S(1)}, bf16[8,112,256]{2,1,0:T(8,128)(2,1)}, u32[]{:S(2)}, u32[]{:S(2)}) collective-permute-start(bf16[8,112,256]{2,1,0:T(8,128)(2,1)S(1)} %all-to-all-done.refs_3_), channel_id=1, source_target_pairs={{0,1},{1,0},{2,3},{3,2},{4,5},{5,4},{6,7},{7,6},{8,9},{9,8},{10,11... | collective-permute-start | bytes 1376264 | tf_op jit(solution)/shard_map/ppermute | solution.py:362
  67.8 35.3 %collective-permute-start.18 = (bf16[8,4,48,256]{3,2,1,0:T(8,128)(2,1)}, bf16[8,4,48,256]{3,2,1,0:T(8,128)(2,1)}, u32[]{:S(2)}, u32[]{:S(2)}) collective-permute-start(bf16[8,4,48,256]{3,2,1,0:T(8,128)(2,1)} %pad_maximum_fusion), channel_id=1, source_target_pairs={{0,12},{1,5},{4,8},{5,1},{8,4},{9,13},{12,0},{13,9},{2,14},{3,7},{... | collective-permute-start | bytes 2359304 | tf_op jit(solution)/shard_map/ppermute | solution.py:353
  69.5 33.6 %collective-permute-start.19 = (bf16[8,4,48,256]{3,2,1,0:T(8,128)(2,1)S(1)}, bf16[8,4,48,256]{3,2,1,0:T(8,128)(2,1)}, u32[]{:S(2)}, u32[]{:S(2)}) collective-permute-start(bf16[8,4,48,256]{3,2,1,0:T(8,128)(2,1)S(1)} %pad_maximum_fusion.1), channel_id=1, source_target_pairs={{0,48},{1,17},{16,32},{17,1},{32,16},{33,49},{48,0},{49,33},{2,50}... | collective-permute-start | bytes 2359304 | tf_op jit(solution)/shard_map/ppermute | solution.py:353
  86.6 0.9 copy-start
  89.2 6.7 %collective-permute-start.16 = (f32[88,128]{1,0:T(8,128)}, f32[88,128]{1,0:T(8,128)S(1)}, u32[]{:S(2)}, u32[]{:S(2)}) collective-permute-start(f32[88,128]{1,0:T(8,128)} %sum.1), channel_id=1, source_target_pairs={{0,0},{1,64},{2,2},{3,66},{16,1},{17,65},{18,3},{19,67},{32,128},{... | collective-permute-start | bytes 135176 | tf_op jit(solution)/shard_map/ppermute | solution.py:435
  96.0 7.2 %copy-start.20 = (f32[88,128]{1,0:T(8,128)}, f32[88,128]{1,0:T(8,128)S(1)}, u32[]{:S(2)}) copy-start(f32[88,128]{1,0:T(8,128)S(1)} %collective-permute-done.16.refs_5_) | copy-start | bytes 135172
  96.0 7.2 %collective-permute-start.17 = (f32[88,128]{1,0:T(8,128)S(1)}, f32[88,128]{1,0:T(8,128)S(1)}, u32[]{:S(2)}, u32[]{:S(2)}) collective-permute-start(f32[88,128]{1,0:T(8,128)S(1)} %collective-permute-done.16.refs_5_), channel_id=1, source_target_pairs={{0,1},{1,0},{2,3},{3,2},{4,5},{5,4},{6,7},{7,6},{8,9},{9,8},{10,11... | collective-permute-start | bytes 135176 | tf_op jit(solution)/shard_map/ppermute | solution.py:436
  103.2 0.6 copy-start.21
  116.9 2.4 %collective-permute-start.20 = (f32[1184,128]{1,0:T(8,128)}, f32[1184,128]{1,0:T(8,128)S(1)}, u32[]{:S(2)}, u32[]{:S(2)}) collective-permute-start(f32[1184,128]{1,0:T(8,128)} %get-tuple-element.75), channel_id=1, source_target_pairs={{0,1},{1,0},{2,3},{3,2},{4,5},{5,4},{6,7},{7,6},{8,9},{9,8},{10,11... | collective-permute-start | bytes 1818632 | tf_op jit(solution)/shard_map/ppermute | solution.py:446
  119.3 0.8 copy-start.5
  143.2 3.4 %copy-start.3 = (bf16[4,32,1152]{2,1,0:T(8,128)(2,1)}, bf16[4,32,1152]{2,1,0:T(8,128)(2,1)S(1)}, u32[]{:S(2)}) copy-start(bf16[4,32,1152]{2,1,0:T(8,128)(2,1)S(1)} %all_to_all.15.near) | copy-start | bytes 884740
  143.2 3.4 %collective-permute-start.21 = (bf16[4,32,1152]{2,1,0:T(8,128)(2,1)S(1)}, bf16[4,32,1152]{2,1,0:T(8,128)(2,1)S(1)}, u32[]{:S(2)}, u32[]{:S(2)}) collective-permute-start(bf16[4,32,1152]{2,1,0:T(8,128)(2,1)S(1)} %all_to_all.15.near), channel_id=1, source_target_pairs={{0,1},{1,0},{2,3},{3,2},{4,5},{5,4},{6,7},{7,6},{8,9},{9,8},{10,11... | collective-permute-start | bytes 884744 | tf_op jit(solution)/shard_map/ppermute | solution.py:457
  146.6 0.7 copy-start.8
